TPU v7x, 256 devices: a whole 4x4x8 slice. The times are simulated.
256 devices in a mesh: section: 16 (over y, x), expert: 16 (over z, core).
Axes of the slice: x: 4, y: 4, z: 8, core: 2. Of those that a mesh axis runs over, the one named last changes fastest.
Arguments:
- acts: bfloat16 [2, 128, 2048], P(None, 'expert'), may hold values from -6 to 6
- norm_gain: float32 [16, 2048], P('section'), may hold values from 0.1 to 1.9
- gate_w: bfloat16 [16, 16, 2048, 768], P('section', 'expert'), may hold values from -0.125 to 0.125
- up_w: bfloat16 [16, 16, 2048, 768], P('section', 'expert'), may hold values from -0.125 to 0.125
- down_w: bfloat16 [16, 16, 768, 2048], P('section', 'expert'), may hold values from -0.21875 to 0.21875
- route_ids: int32 [16, 2, 128, 2], P('section', None, 'expert'), may hold values from 0 to 15, all different within a row; in each aligned block of 8 rows (0 to 7, 8 to 15, ..., all dimensions but the last counted through in order) at most 2 rows name the same one
- route_probs: float32 [16, 2, 128, 2], P('section', None, 'expert'), may hold values from 0.2 to 1
Outputs:
- layer_outputs: float32 [16, 2, 128, 2048], P('section', None, 'expert')
- hessians: float32 [16, 16, 768, 768], P('section', 'expert')
Inputs may be any that keep to these rules, and one draw needn't show every extreme that they name: `route_ids`: each token names 2 different experts; in one layer and micro-batch the 8 tokens of one index of expert name one expert at most 2 times, a bound that some block reaches in some of these groups.
All inputs are finite; a program needn't handle non-finite values.
Results may differ from a plain program's by a relative error of at most 0.04.
Values may be sent and summed in bfloat16 or wider, within the bound.
No kernel may reach another device: no remote copies, remote signals or barrier semaphores. Data moves between devices by JAX's collectives and lax.ppermute only.
A program may use at most 64 MiB of HBM per device.

v0:
```python
import jax
import jax.numpy as jnp
from jax import lax
from jax.sharding import PartitionSpec as P


def shifted(value, axis, steps):
    count = lax.axis_size(axis)
    leading, last = (max(0, -steps), min(count, count - steps))
    return lax.ppermute(value, axis, [(source, source + steps) for source in range(leading, last)])


def slot_numbers(chosen, experts):
    count = chosen.shape[-1]
    onehot = (chosen[..., None] == jnp.arange(experts, dtype=jnp.int32)).astype(jnp.float32)
    lower = (jnp.arange(count)[:, None] > jnp.arange(count)[None, :]).astype(jnp.float32)
    before = jnp.einsum("ij,...je->...ie", lower, onehot, precision=lax.Precision.HIGHEST)
    return jnp.sum(before * onehot, axis=-1).astype(jnp.int32)


def body(acts, norm_gain, gate_w, up_w, down_w, route_ids, route_probs):
    sections = lax.axis_size("section")
    section = lax.axis_index("section")
    owners = lax.axis_size("expert")
    batches, tok_rows, feature = acts.shape
    picks = route_ids.shape[-1]
    assigns = tok_rows * picks
    hidden_width = gate_w.shape[-1]
    capacity = max(2, (3 * assigns + 2 * owners - 1) // (2 * owners))
    slots_all = owners * capacity
    scale = 2.0 / (batches * assigns)
    gain = norm_gain[0]
    w_gate = gate_w[0, 0]
    w_up = up_w[0, 0]
    w_down = down_w[0, 0]
    chosen_all = route_ids[0]
    weights_all = route_probs[0]
    contract_rows = (((0,), (0,)), ((), ()))

    def expert_apply(rows):
        gate = jnp.dot(rows, w_gate, preferred_element_type=jnp.float32)
        upper = jnp.dot(rows, w_up, preferred_element_type=jnp.float32)
        hidden = (jax.nn.silu(gate) * upper).astype(jnp.bfloat16)
        return (
            jnp.dot(hidden, w_down, preferred_element_type=jnp.float32).astype(jnp.bfloat16),
            hidden,
        )

    def tick(step, carry):
        arrived, layer_out, store = carry
        batch = step - section
        active = (batch >= 0) & (batch < batches)
        held = jnp.clip(batch, 0, batches - 1)
        fresh = lax.dynamic_index_in_dim(
            acts, jnp.clip(step, 0, batches - 1), 0, keepdims=False
        ).astype(jnp.float32)
        wide = jnp.where(section == 0, fresh, arrived)
        normed = (
            wide * lax.rsqrt(jnp.mean(wide * wide, axis=-1, keepdims=True) + 1e-06) * gain
        ).astype(jnp.bfloat16)
        chosen = lax.dynamic_index_in_dim(chosen_all, held, 0, keepdims=False)
        weights = lax.dynamic_index_in_dim(weights_all, held, 0, keepdims=False)
        flat = chosen.reshape(assigns)
        slot = slot_numbers(flat, owners)
        target = flat * capacity + slot
        dispatch_map = (jnp.arange(slots_all, dtype=jnp.int32)[:, None] == target[None, :]).astype(
            jnp.bfloat16
        )
        spread = jnp.repeat(normed, picks, axis=0)
        outgoing = jnp.dot(dispatch_map, spread, preferred_element_type=jnp.float32).astype(
            jnp.bfloat16
        )
        outgoing = outgoing.reshape(owners, capacity, feature)
        incoming = lax.all_to_all(outgoing, "expert", split_axis=0, concat_axis=0, tiled=True)
        senders = incoming.shape[0]
        count = incoming.shape[1]
        output, hidden = expert_apply(incoming.reshape(senders * count, feature))
        back = lax.all_to_all(
            output.reshape(senders, count, feature),
            "expert",
            split_axis=0,
            concat_axis=0,
            tiled=True,
        )
        hidden_three = hidden.reshape(senders, count, hidden_width)
        hidden_rows = hidden_three.reshape(slots_all, hidden_width)
        picked = lax.dot_general(
            dispatch_map,
            back.reshape(slots_all, feature),
            contract_rows,
            preferred_element_type=jnp.float32,
        )
        picked = picked.reshape(tok_rows, picks, feature)
        mixed = jnp.sum(weights[..., None] * picked, axis=1)
        result = wide + mixed
        passed = shifted(result, "section", 1)
        previous = lax.dynamic_index_in_dim(layer_out, held, 0, keepdims=False)
        layer_out = lax.dynamic_update_index_in_dim(
            layer_out, jnp.where(active, result, previous), held, 0
        )
        square = lax.dot_general(
            hidden_rows, hidden_rows, contract_rows, preferred_element_type=jnp.float32
        )
        store = store + jnp.where(active, square, 0.0)
        return (passed, layer_out, store)

    arrived = jnp.zeros((tok_rows, feature), jnp.float32)
    layer_out = jnp.zeros((batches, tok_rows, feature), jnp.float32)
    store = jnp.zeros((hidden_width, hidden_width), jnp.float32)
    arrived, layer_out, store = lax.fori_loop(
        0, batches + sections - 1, tick, (arrived, layer_out, store)
    )
    hessian = scale * store
    return (layer_out[None], hessian[None, None])


def solution(mesh):
    placed = (
        P(None, "expert", None),
        P("section", None),
        P("section", "expert", None, None),
        P("section", "expert", None, None),
        P("section", "expert", None, None),
        P("section", None, "expert", None),
        P("section", None, "expert", None),
    )
    return jax.shard_map(
        body,
        mesh=mesh,
        in_specs=placed,
        out_specs=(P("section", None, "expert", None), P("section", "expert", None, None)),
        check_vma=False,
    )
```

profile of v0, /device:TPU:16, one launch (start us, length us, event | category | flops | bytes accessed | tf_op | source)
XLA Modules:
  0.0 738.8 jit_solution(275290602799263683)
XLA Ops:
  0.7 736.5 %while.19 = (s32[]{:T(128)}, f32[8,2048]{1,0:T(8,128)S(1)}, f32[2,8,2048]{2,1,0:T(8,128)S(1)}, f32[768,768]{1,0:T(8,128)S(1)}, pred[]{:T(512)}, /*index=5*/bf16[...) while((s32[]{:T(128)}, f32[8,2048]{1,0:T(8,128)S(1)}, ...), condition=%wide.region_4.5_spmd.clone, body=%wide.region_0.4_spmd.clone.sunk | while | flops 346253632 | bytes 43774064 | solution.py:110
  13.1 8.7 %all-to-all-done = bf16[16,2,2048]{2,1,0:T(2,128)(2,1)S(1)} async-done(((bf16[16,2,2048]{2,1,0:T(2,128)(2,1)}), bf16[16,2,2048]{2,1,0:T(2,128)(2,1)S(1)}, u32[]{:S(2)}, u32[]{:S(2)}) %all-to-all-start) | async-done | bytes 131104 | tf_op jit(solution)/shard_map/while/body/eval_jaxpr/all_to_all | solution.py:74
  31.5 8.6 %all-to-all-done.1 = bf16[16,2,2048]{2,1,0:T(2,128)(2,1)S(1)} async-done(((bf16[16,2,2048]{2,1,0:T(2,128)(2,1)}), bf16[16,2,2048]{2,1,0:T(2,128)(2,1)S(1)}, u32[]{:S(2)}, u32[]{:S(2)}) %all-to-all-start.1) | async-done | bytes 131104 | tf_op jit(solution)/shard_map/while/body/eval_jaxpr/all_to_all | solution.py:78
  56.2 8.6 %all-to-all-done = bf16[16,2,2048]{2,1,0:T(2,128)(2,1)S(1)} async-done(((bf16[16,2,2048]{2,1,0:T(2,128)(2,1)}), bf16[16,2,2048]{2,1,0:T(2,128)(2,1)S(1)}, u32[]{:S(2)}, u32[]{:S(2)}) %all-to-all-start) | async-done | bytes 131104 | tf_op jit(solution)/shard_map/while/body/eval_jaxpr/all_to_all | solution.py:74
  74.5 8.6 %all-to-all-done.1 = bf16[16,2,2048]{2,1,0:T(2,128)(2,1)S(1)} async-done(((bf16[16,2,2048]{2,1,0:T(2,128)(2,1)}), bf16[16,2,2048]{2,1,0:T(2,128)(2,1)S(1)}, u32[]{:S(2)}, u32[]{:S(2)}) %all-to-all-start.1) | async-done | bytes 131104 | tf_op jit(solution)/shard_map/while/body/eval_jaxpr/all_to_all | solution.py:78
  99.2 8.6 %all-to-all-done = bf16[16,2,2048]{2,1,0:T(2,128)(2,1)S(1)} async-done(((bf16[16,2,2048]{2,1,0:T(2,128)(2,1)}), bf16[16,2,2048]{2,1,0:T(2,128)(2,1)S(1)}, u32[]{:S(2)}, u32[]{:S(2)}) %all-to-all-start) | async-done | bytes 131104 | tf_op jit(solution)/shard_map/while/body/eval_jaxpr/all_to_all | solution.py:74
  117.5 8.6 %all-to-all-done.1 = bf16[16,2,2048]{2,1,0:T(2,128)(2,1)S(1)} async-done(((bf16[16,2,2048]{2,1,0:T(2,128)(2,1)}), bf16[16,2,2048]{2,1,0:T(2,128)(2,1)S(1)}, u32[]{:S(2)}, u32[]{:S(2)}) %all-to-all-start.1) | async-done | bytes 131104 | tf_op jit(solution)/shard_map/while/body/eval_jaxpr/all_to_all | solution.py:78
  142.2 8.6 %all-to-all-done = bf16[16,2,2048]{2,1,0:T(2,128)(2,1)S(1)} async-done(((bf16[16,2,2048]{2,1,0:T(2,128)(2,1)}), bf16[16,2,2048]{2,1,0:T(2,128)(2,1)S(1)}, u32[]{:S(2)}, u32[]{:S(2)}) %all-to-all-start) | async-done | bytes 131104 | tf_op jit(solution)/shard_map/while/body/eval_jaxpr/all_to_all | solution.py:74
  160.5 8.6 %all-to-all-done.1 = bf16[16,2,2048]{2,1,0:T(2,128)(2,1)S(1)} async-done(((bf16[16,2,2048]{2,1,0:T(2,128)(2,1)}), bf16[16,2,2048]{2,1,0:T(2,128)(2,1)S(1)}, u32[]{:S(2)}, u32[]{:S(2)}) %all-to-all-start.1) | async-done | bytes 131104 | tf_op jit(solution)/shard_map/while/body/eval_jaxpr/all_to_all | solution.py:78
  185.3 8.6 %all-to-all-done = bf16[16,2,2048]{2,1,0:T(2,128)(2,1)S(1)} async-done(((bf16[16,2,2048]{2,1,0:T(2,128)(2,1)}), bf16[16,2,2048]{2,1,0:T(2,128)(2,1)S(1)}, u32[]{:S(2)}, u32[]{:S(2)}) %all-to-all-start) | async-done | bytes 131104 | tf_op jit(solution)/shard_map/while/body/eval_jaxpr/all_to_all | solution.py:74
  203.6 8.6 %all-to-all-done.1 = bf16[16,2,2048]{2,1,0:T(2,128)(2,1)S(1)} async-done(((bf16[16,2,2048]{2,1,0:T(2,128)(2,1)}), bf16[16,2,2048]{2,1,0:T(2,128)(2,1)S(1)}, u32[]{:S(2)}, u32[]{:S(2)}) %all-to-all-start.1) | async-done | bytes 131104 | tf_op jit(solution)/shard_map/while/body/eval_jaxpr/all_to_all | solution.py:78
  228.3 8.6 %all-to-all-done = bf16[16,2,2048]{2,1,0:T(2,128)(2,1)S(1)} async-done(((bf16[16,2,2048]{2,1,0:T(2,128)(2,1)}), bf16[16,2,2048]{2,1,0:T(2,128)(2,1)S(1)}, u32[]{:S(2)}, u32[]{:S(2)}) %all-to-all-start) | async-done | bytes 131104 | tf_op jit(solution)/shard_map/while/body/eval_jaxpr/all_to_all | solution.py:74
  271.3 8.6 %all-to-all-done = bf16[16,2,2048]{2,1,0:T(2,128)(2,1)S(1)} async-done(((bf16[16,2,2048]{2,1,0:T(2,128)(2,1)}), bf16[16,2,2048]{2,1,0:T(2,128)(2,1)S(1)}, u32[]{:S(2)}, u32[]{:S(2)}) %all-to-all-start) | async-done | bytes 131104 | tf_op jit(solution)/shard_map/while/body/eval_jaxpr/all_to_all | solution.py:74
  314.3 8.6 %all-to-all-done = bf16[16,2,2048]{2,1,0:T(2,128)(2,1)S(1)} async-done(((bf16[16,2,2048]{2,1,0:T(2,128)(2,1)}), bf16[16,2,2048]{2,1,0:T(2,128)(2,1)S(1)}, u32[]{:S(2)}, u32[]{:S(2)}) %all-to-all-start) | async-done | bytes 131104 | tf_op jit(solution)/shard_map/while/body/eval_jaxpr/all_to_all | solution.py:74
  357.4 8.6 %all-to-all-done = bf16[16,2,2048]{2,1,0:T(2,128)(2,1)S(1)} async-done(((bf16[16,2,2048]{2,1,0:T(2,128)(2,1)}), bf16[16,2,2048]{2,1,0:T(2,128)(2,1)S(1)}, u32[]{:S(2)}, u32[]{:S(2)}) %all-to-all-start) | async-done | bytes 131104 | tf_op jit(solution)/shard_map/while/body/eval_jaxpr/all_to_all | solution.py:74
  400.4 8.6 %all-to-all-done = bf16[16,2,2048]{2,1,0:T(2,128)(2,1)S(1)} async-done(((bf16[16,2,2048]{2,1,0:T(2,128)(2,1)}), bf16[16,2,2048]{2,1,0:T(2,128)(2,1)S(1)}, u32[]{:S(2)}, u32[]{:S(2)}) %all-to-all-start) | async-done | bytes 131104 | tf_op jit(solution)/shard_map/while/body/eval_jaxpr/all_to_all | solution.py:74
  443.4 8.6 %all-to-all-done = bf16[16,2,2048]{2,1,0:T(2,128)(2,1)S(1)} async-done(((bf16[16,2,2048]{2,1,0:T(2,128)(2,1)}), bf16[16,2,2048]{2,1,0:T(2,128)(2,1)S(1)}, u32[]{:S(2)}, u32[]{:S(2)}) %all-to-all-start) | async-done | bytes 131104 | tf_op jit(solution)/shard_map/while/body/eval_jaxpr/all_to_all | solution.py:74
  486.4 8.6 %all-to-all-done = bf16[16,2,2048]{2,1,0:T(2,128)(2,1)S(1)} async-done(((bf16[16,2,2048]{2,1,0:T(2,128)(2,1)}), bf16[16,2,2048]{2,1,0:T(2,128)(2,1)S(1)}, u32[]{:S(2)}, u32[]{:S(2)}) %all-to-all-start) | async-done | bytes 131104 | tf_op jit(solution)/shard_map/while/body/eval_jaxpr/all_to_all | solution.py:74
  504.7 8.6 %all-to-all-done.1 = bf16[16,2,2048]{2,1,0:T(2,128)(2,1)S(1)} async-done(((bf16[16,2,2048]{2,1,0:T(2,128)(2,1)}), bf16[16,2,2048]{2,1,0:T(2,128)(2,1)S(1)}, u32[]{:S(2)}, u32[]{:S(2)}) %all-to-all-start.1) | async-done | bytes 131104 | tf_op jit(solution)/shard_map/while/body/eval_jaxpr/all_to_all | solution.py:78
  529.5 8.6 %all-to-all-done = bf16[16,2,2048]{2,1,0:T(2,128)(2,1)S(1)} async-done(((bf16[16,2,2048]{2,1,0:T(2,128)(2,1)}), bf16[16,2,2048]{2,1,0:T(2,128)(2,1)S(1)}, u32[]{:S(2)}, u32[]{:S(2)}) %all-to-all-start) | async-done | bytes 131104 | tf_op jit(solution)/shard_map/while/body/eval_jaxpr/all_to_all | solution.py:74
  572.5 8.6 %all-to-all-done = bf16[16,2,2048]{2,1,0:T(2,128)(2,1)S(1)} async-done(((bf16[16,2,2048]{2,1,0:T(2,128)(2,1)}), bf16[16,2,2048]{2,1,0:T(2,128)(2,1)S(1)}, u32[]{:S(2)}, u32[]{:S(2)}) %all-to-all-start) | async-done | bytes 131104 | tf_op jit(solution)/shard_map/while/body/eval_jaxpr/all_to_all | solution.py:74
  615.5 8.6 %all-to-all-done = bf16[16,2,2048]{2,1,0:T(2,128)(2,1)S(1)} async-done(((bf16[16,2,2048]{2,1,0:T(2,128)(2,1)}), bf16[16,2,2048]{2,1,0:T(2,128)(2,1)S(1)}, u32[]{:S(2)}, u32[]{:S(2)}) %all-to-all-start) | async-done | bytes 131104 | tf_op jit(solution)/shard_map/while/body/eval_jaxpr/all_to_all | solution.py:74
  658.5 8.6 %all-to-all-done = bf16[16,2,2048]{2,1,0:T(2,128)(2,1)S(1)} async-done(((bf16[16,2,2048]{2,1,0:T(2,128)(2,1)}), bf16[16,2,2048]{2,1,0:T(2,128)(2,1)S(1)}, u32[]{:S(2)}, u32[]{:S(2)}) %all-to-all-start) | async-done | bytes 131104 | tf_op jit(solution)/shard_map/while/body/eval_jaxpr/all_to_all | solution.py:74
  701.5 8.6 %all-to-all-done = bf16[16,2,2048]{2,1,0:T(2,128)(2,1)S(1)} async-done(((bf16[16,2,2048]{2,1,0:T(2,128)(2,1)}), bf16[16,2,2048]{2,1,0:T(2,128)(2,1)S(1)}, u32[]{:S(2)}, u32[]{:S(2)}) %all-to-all-start) | async-done | bytes 131104 | tf_op jit(solution)/shard_map/while/body/eval_jaxpr/all_to_all | solution.py:74
  (646 shorter events, 537.5 us)
Async XLA Ops:
  4.5 17.3 %all-to-all-start = ((bf16[16,2,2048]{2,1,0:T(2,128)(2,1)}), bf16[16,2,2048]{2,1,0:T(2,128)(2,1)S(1)}, u32[]{:S(2)}, u32[]{:S(2)}) async-start(bf16[16,2,2048]{2,1,0:T(2,128)(2,1)} %reshape.134), calls=%async_computation | async-start | bytes 262144 | tf_op jit(solution)/shard_map/while/body/eval_jaxpr/all_to_all | solution.py:74
  27.9 12.2 %all-to-all-start.1 = ((bf16[16,2,2048]{2,1,0:T(2,128)(2,1)}), bf16[16,2,2048]{2,1,0:T(2,128)(2,1)S(1)}, u32[]{:S(2)}, u32[]{:S(2)}) async-start(bf16[16,2,2048]{2,1,0:T(2,128)(2,1)} %reshape.136), calls=%async_computation.1 | async-start | bytes 262144 | tf_op jit(solution)/shard_map/while/body/eval_jaxpr/all_to_all | solution.py:78
  52.6 12.2 %all-to-all-start = ((bf16[16,2,2048]{2,1,0:T(2,128)(2,1)}), bf16[16,2,2048]{2,1,0:T(2,128)(2,1)S(1)}, u32[]{:S(2)}, u32[]{:S(2)}) async-start(bf16[16,2,2048]{2,1,0:T(2,128)(2,1)} %reshape.134), calls=%async_computation | async-start | bytes 262144 | tf_op jit(solution)/shard_map/while/body/eval_jaxpr/all_to_all | solution.py:74
  70.9 12.2 %all-to-all-start.1 = ((bf16[16,2,2048]{2,1,0:T(2,128)(2,1)}), bf16[16,2,2048]{2,1,0:T(2,128)(2,1)S(1)}, u32[]{:S(2)}, u32[]{:S(2)}) async-start(bf16[16,2,2048]{2,1,0:T(2,128)(2,1)} %reshape.136), calls=%async_computation.1 | async-start | bytes 262144 | tf_op jit(solution)/shard_map/while/body/eval_jaxpr/all_to_all | solution.py:78
  95.6 12.2 %all-to-all-start = ((bf16[16,2,2048]{2,1,0:T(2,128)(2,1)}), bf16[16,2,2048]{2,1,0:T(2,128)(2,1)S(1)}, u32[]{:S(2)}, u32[]{:S(2)}) async-start(bf16[16,2,2048]{2,1,0:T(2,128)(2,1)} %reshape.134), calls=%async_computation | async-start | bytes 262144 | tf_op jit(solution)/shard_map/while/body/eval_jaxpr/all_to_all | solution.py:74
  113.9 12.2 %all-to-all-start.1 = ((bf16[16,2,2048]{2,1,0:T(2,128)(2,1)}), bf16[16,2,2048]{2,1,0:T(2,128)(2,1)S(1)}, u32[]{:S(2)}, u32[]{:S(2)}) async-start(bf16[16,2,2048]{2,1,0:T(2,128)(2,1)} %reshape.136), calls=%async_computation.1 | async-start | bytes 262144 | tf_op jit(solution)/shard_map/while/body/eval_jaxpr/all_to_all | solution.py:78
  138.6 12.2 %all-to-all-start = ((bf16[16,2,2048]{2,1,0:T(2,128)(2,1)}), bf16[16,2,2048]{2,1,0:T(2,128)(2,1)S(1)}, u32[]{:S(2)}, u32[]{:S(2)}) async-start(bf16[16,2,2048]{2,1,0:T(2,128)(2,1)} %reshape.134), calls=%async_computation | async-start | bytes 262144 | tf_op jit(solution)/shard_map/while/body/eval_jaxpr/all_to_all | solution.py:74
  156.9 12.2 %all-to-all-start.1 = ((bf16[16,2,2048]{2,1,0:T(2,128)(2,1)}), bf16[16,2,2048]{2,1,0:T(2,128)(2,1)S(1)}, u32[]{:S(2)}, u32[]{:S(2)}) async-start(bf16[16,2,2048]{2,1,0:T(2,128)(2,1)} %reshape.136), calls=%async_computation.1 | async-start | bytes 262144 | tf_op jit(solution)/shard_map/while/body/eval_jaxpr/all_to_all | solution.py:78
  181.7 12.2 %all-to-all-start = ((bf16[16,2,2048]{2,1,0:T(2,128)(2,1)}), bf16[16,2,2048]{2,1,0:T(2,128)(2,1)S(1)}, u32[]{:S(2)}, u32[]{:S(2)}) async-start(bf16[16,2,2048]{2,1,0:T(2,128)(2,1)} %reshape.134), calls=%async_computation | async-start | bytes 262144 | tf_op jit(solution)/shard_map/while/body/eval_jaxpr/all_to_all | solution.py:74
  200.0 12.2 %all-to-all-start.1 = ((bf16[16,2,2048]{2,1,0:T(2,128)(2,1)}), bf16[16,2,2048]{2,1,0:T(2,128)(2,1)S(1)}, u32[]{:S(2)}, u32[]{:S(2)}) async-start(bf16[16,2,2048]{2,1,0:T(2,128)(2,1)} %reshape.136), calls=%async_computation.1 | async-start | bytes 262144 | tf_op jit(solution)/shard_map/while/body/eval_jaxpr/all_to_all | solution.py:78
  224.7 12.2 %all-to-all-start = ((bf16[16,2,2048]{2,1,0:T(2,128)(2,1)}), bf16[16,2,2048]{2,1,0:T(2,128)(2,1)S(1)}, u32[]{:S(2)}, u32[]{:S(2)}) async-start(bf16[16,2,2048]{2,1,0:T(2,128)(2,1)} %reshape.134), calls=%async_computation | async-start | bytes 262144 | tf_op jit(solution)/shard_map/while/body/eval_jaxpr/all_to_all | solution.py:74
  243.0 12.2 %all-to-all-start.1 = ((bf16[16,2,2048]{2,1,0:T(2,128)(2,1)}), bf16[16,2,2048]{2,1,0:T(2,128)(2,1)S(1)}, u32[]{:S(2)}, u32[]{:S(2)}) async-start(bf16[16,2,2048]{2,1,0:T(2,128)(2,1)} %reshape.136), calls=%async_computation.1 | async-start | bytes 262144 | tf_op jit(solution)/shard_map/while/body/eval_jaxpr/all_to_all | solution.py:78
  267.7 12.2 %all-to-all-start = ((bf16[16,2,2048]{2,1,0:T(2,128)(2,1)}), bf16[16,2,2048]{2,1,0:T(2,128)(2,1)S(1)}, u32[]{:S(2)}, u32[]{:S(2)}) async-start(bf16[16,2,2048]{2,1,0:T(2,128)(2,1)} %reshape.134), calls=%async_computation | async-start | bytes 262144 | tf_op jit(solution)/shard_map/while/body/eval_jaxpr/all_to_all | solution.py:74
  286.0 12.2 %all-to-all-start.1 = ((bf16[16,2,2048]{2,1,0:T(2,128)(2,1)}), bf16[16,2,2048]{2,1,0:T(2,128)(2,1)S(1)}, u32[]{:S(2)}, u32[]{:S(2)}) async-start(bf16[16,2,2048]{2,1,0:T(2,128)(2,1)} %reshape.136), calls=%async_computation.1 | async-start | bytes 262144 | tf_op jit(solution)/shard_map/while/body/eval_jaxpr/all_to_all | solution.py:78
  310.7 12.2 %all-to-all-start = ((bf16[16,2,2048]{2,1,0:T(2,128)(2,1)}), bf16[16,2,2048]{2,1,0:T(2,128)(2,1)S(1)}, u32[]{:S(2)}, u32[]{:S(2)}) async-start(bf16[16,2,2048]{2,1,0:T(2,128)(2,1)} %reshape.134), calls=%async_computation | async-start | bytes 262144 | tf_op jit(solution)/shard_map/while/body/eval_jaxpr/all_to_all | solution.py:74
  353.8 12.2 %all-to-all-start = ((bf16[16,2,2048]{2,1,0:T(2,128)(2,1)}), bf16[16,2,2048]{2,1,0:T(2,128)(2,1)S(1)}, u32[]{:S(2)}, u32[]{:S(2)}) async-start(bf16[16,2,2048]{2,1,0:T(2,128)(2,1)} %reshape.134), calls=%async_computation | async-start | bytes 262144 | tf_op jit(solution)/shard_map/while/body/eval_jaxpr/all_to_all | solution.py:74
  396.8 12.2 %all-to-all-start = ((bf16[16,2,2048]{2,1,0:T(2,128)(2,1)}), bf16[16,2,2048]{2,1,0:T(2,128)(2,1)S(1)}, u32[]{:S(2)}, u32[]{:S(2)}) async-start(bf16[16,2,2048]{2,1,0:T(2,128)(2,1)} %reshape.134), calls=%async_computation | async-start | bytes 262144 | tf_op jit(solution)/shard_map/while/body/eval_jaxpr/all_to_all | solution.py:74
  439.8 12.2 %all-to-all-start = ((bf16[16,2,2048]{2,1,0:T(2,128)(2,1)}), bf16[16,2,2048]{2,1,0:T(2,128)(2,1)S(1)}, u32[]{:S(2)}, u32[]{:S(2)}) async-start(bf16[16,2,2048]{2,1,0:T(2,128)(2,1)} %reshape.134), calls=%async_computation | async-start | bytes 262144 | tf_op jit(solution)/shard_map/while/body/eval_jaxpr/all_to_all | solution.py:74
  482.8 12.2 %all-to-all-start = ((bf16[16,2,2048]{2,1,0:T(2,128)(2,1)}), bf16[16,2,2048]{2,1,0:T(2,128)(2,1)S(1)}, u32[]{:S(2)}, u32[]{:S(2)}) async-start(bf16[16,2,2048]{2,1,0:T(2,128)(2,1)} %reshape.134), calls=%async_computation | async-start | bytes 262144 | tf_op jit(solution)/shard_map/while/body/eval_jaxpr/all_to_all | solution.py:74
  525.9 12.2 %all-to-all-start = ((bf16[16,2,2048]{2,1,0:T(2,128)(2,1)}), bf16[16,2,2048]{2,1,0:T(2,128)(2,1)S(1)}, u32[]{:S(2)}, u32[]{:S(2)}) async-start(bf16[16,2,2048]{2,1,0:T(2,128)(2,1)} %reshape.134), calls=%async_computation | async-start | bytes 262144 | tf_op jit(solution)/shard_map/while/body/eval_jaxpr/all_to_all | solution.py:74
  568.9 12.2 %all-to-all-start = ((bf16[16,2,2048]{2,1,0:T(2,128)(2,1)}), bf16[16,2,2048]{2,1,0:T(2,128)(2,1)S(1)}, u32[]{:S(2)}, u32[]{:S(2)}) async-start(bf16[16,2,2048]{2,1,0:T(2,128)(2,1)} %reshape.134), calls=%async_computation | async-start | bytes 262144 | tf_op jit(solution)/shard_map/while/body/eval_jaxpr/all_to_all | solution.py:74
  611.9 12.2 %all-to-all-start = ((bf16[16,2,2048]{2,1,0:T(2,128)(2,1)}), bf16[16,2,2048]{2,1,0:T(2,128)(2,1)S(1)}, u32[]{:S(2)}, u32[]{:S(2)}) async-start(bf16[16,2,2048]{2,1,0:T(2,128)(2,1)} %reshape.134), calls=%async_computation | async-start | bytes 262144 | tf_op jit(solution)/shard_map/while/body/eval_jaxpr/all_to_all | solution.py:74
  654.9 12.2 %all-to-all-start = ((bf16[16,2,2048]{2,1,0:T(2,128)(2,1)}), bf16[16,2,2048]{2,1,0:T(2,128)(2,1)S(1)}, u32[]{:S(2)}, u32[]{:S(2)}) async-start(bf16[16,2,2048]{2,1,0:T(2,128)(2,1)} %reshape.134), calls=%async_computation | async-start | bytes 262144 | tf_op jit(solution)/shard_map/while/body/eval_jaxpr/all_to_all | solution.py:74
  698.0 12.2 %all-to-all-start = ((bf16[16,2,2048]{2,1,0:T(2,128)(2,1)}), bf16[16,2,2048]{2,1,0:T(2,128)(2,1)S(1)}, u32[]{:S(2)}, u32[]{:S(2)}) async-start(bf16[16,2,2048]{2,1,0:T(2,128)(2,1)} %reshape.134), calls=%async_computation | async-start | bytes 262144 | tf_op jit(solution)/shard_map/while/body/eval_jaxpr/all_to_all | solution.py:74
  (96 other events, 707.2 us)
where the time goes:
time: 745 us; the launch traced here: 739 us
  waiting for transfers between devices  388 us (52%)
  starting transfers between devices  159 us (21%)
  matrix products  89.9 us (12%)
  local copies, waits for them, and re-layouts  66.4 us (9%)
  other arithmetic  33.2 us (4%)
    all_to_all x17, waiting for transfers between devices, tick(): lax.all_to_all(outgoing, 'expert', split_axis=0, concat_axis=0, tiled=True)  147 us
    all_to_all x17, waiting for transfers between devices, tick(): lax.all_to_all(output.reshape(senders, count, feature), 'expert', split_a...  146 us
    ppermute x17, waiting for transfers between devices, shifted(): lax.ppermute(value, axis, [(source, source + steps) for source in range(l...  95 us
    all_to_all x17, starting transfers between devices, tick(): lax.all_to_all(outgoing, 'expert', split_axis=0, concat_axis=0, tiled=True)  64.8 us
    all_to_all x17, starting transfers between devices, tick(): lax.all_to_all(output.reshape(senders, count, feature), 'expert', split_a...  59.7 us
    dot_general x17, matrix products, expert_apply(): gate = jnp.dot(rows, w_gate, preferred_element_type=jnp.float32)  45.2 us
    ppermute x17, starting transfers between devices, shifted(): lax.ppermute(value, axis, [(source, source + steps) for source in range(l...  34.1 us
    while x136, local copies, waits for them, and re-layouts  22.2 us
  transfers between devices with their start and end apart: 51, of which 51 were waited for; matrix products, arithmetic and copies ran while one was open for 2% of the time, Pallas kernels for 0%

commit v1 on v0

v1 whole, which is shorter than its diff:
```python
import functools

import jax
import jax.numpy as jnp
from jax import lax
from jax.experimental import pallas as pl
from jax.experimental.pallas import tpu as pltpu
from jax.sharding import PartitionSpec as P

LANES = 128
SLOTS = 2
BF16 = jnp.bfloat16
F32 = jnp.float32


def vmem():
    return pl.BlockSpec(memory_space=pltpu.VMEM)


def smem():
    return pl.BlockSpec(memory_space=pltpu.SMEM)


def spread_rows(rows, spare, owners):
    blocks = rows.shape[1] // LANES
    for slot in range(SLOTS):
        for block in range(blocks):
            spare[pl.ds(slot * blocks + block, owners, stride=SLOTS * blocks), :] = rows[
                slot * owners : (slot + 1) * owners, block * LANES : (block + 1) * LANES
            ]


def gather_rows(spare, owners, blocks):
    parts = []
    for slot in range(SLOTS):
        parts.append(
            jnp.concatenate(
                [
                    spare[pl.ds(slot * blocks + block, owners, stride=SLOTS * blocks), :]
                    for block in range(blocks)
                ],
                axis=1,
            )
        )
    return jnp.concatenate(parts, axis=0)


def tables_kernel(owners, ids_ref, probs_ref, send_ref, take_ref):
    batches, tokens, picks = ids_ref.shape
    experts = lax.broadcasted_iota(jnp.int32, (tokens, owners), 1)
    earlier = (
        lax.broadcasted_iota(jnp.int32, (tokens, tokens), 0)
        > lax.broadcasted_iota(jnp.int32, (tokens, tokens), 1)
    ).astype(BF16)
    for batch in range(batches):
        ids = ids_ref[batch]
        probs = probs_ref[batch]
        named = jnp.zeros((tokens, owners), F32)
        weight = jnp.zeros((tokens, owners), F32)
        for pick in range(picks):
            hit = ids[:, pick : pick + 1] == experts
            named = named + jnp.where(hit, 1.0, 0.0)
            weight = weight + jnp.where(hit, probs[:, pick : pick + 1], 0.0)
        slot = jnp.dot(earlier, named.astype(BF16), preferred_element_type=F32)
        split = [jnp.abs(slot - number) < 0.5 for number in range(SLOTS)]
        send = jnp.concatenate([jnp.where(own, named, 0.0) for own in split], axis=1)
        take = jnp.concatenate([jnp.where(own, weight, 0.0) for own in split], axis=1)
        send_ref[batch] = send.astype(BF16)
        high = take.astype(BF16).astype(F32)
        take_ref[batch] = jnp.concatenate([high, take - high], axis=0).astype(BF16)


def dispatch_kernel(step, owners, held_ref, x_ref, gain_ref, send_ref, out_ref, spare):
    wide = x_ref[...].astype(F32)
    mean = jnp.mean(wide * wide, axis=-1, keepdims=True)
    normed = (wide * lax.rsqrt(mean + 1e-06) * gain_ref[...]).astype(BF16)
    rows = lax.dot_general(
        send_ref[held_ref[step]], normed, (((0,), (0,)), ((), ())), preferred_element_type=F32
    )
    spread_rows(rows, spare, owners)
    out_ref[...] = spare[...].astype(BF16).reshape(out_ref.shape)


def expert_kernel(in_ref, gate_ref, up_ref, down_ref, out_ref, hidden_ref, spare):
    owners, height, lanes = in_ref.shape
    spare[...] = in_ref[...].astype(F32).reshape(owners * height, lanes)
    rows = gather_rows(spare, owners, height // SLOTS).astype(BF16)
    gate = jnp.dot(rows, gate_ref[...], preferred_element_type=F32)
    upper = jnp.dot(rows, up_ref[...], preferred_element_type=F32)
    hidden = (gate / (1.0 + jnp.exp(-gate)) * upper).astype(BF16)
    hidden_ref[...] = hidden
    output = jnp.dot(hidden, down_ref[...], preferred_element_type=F32)
    spread_rows(output, spare, owners)
    out_ref[...] = spare[...].astype(BF16).reshape(out_ref.shape)


def combine_kernel(step, held_ref, x_ref, back_ref, take_ref, out_ref, sent_ref, spare):
    owners, height, lanes = back_ref.shape
    tokens = x_ref.shape[0]
    spare[...] = back_ref[...].astype(F32).reshape(owners * height, lanes)
    rows = gather_rows(spare, owners, height // SLOTS).astype(BF16)
    mixed = jnp.dot(take_ref[held_ref[step]], rows, preferred_element_type=F32)
    result = x_ref[...].astype(F32) + (mixed[:tokens] + mixed[tokens:])
    out_ref[...] = result
    sent_ref[...] = result.astype(BF16)


def body(acts, norm_gain, gate_w, up_w, down_w, route_ids, route_probs):
    sections = lax.axis_size("section")
    section = lax.axis_index("section")
    owners = lax.axis_size("expert")
    batches, tokens, feature = acts.shape
    picks = route_ids.shape[-1]
    hidden_width = gate_w.shape[-1]
    steps = batches + sections - 1
    height = SLOTS * feature // LANES
    scale = 2.0 / (batches * tokens * picks)
    w_gate, w_up, w_down = gate_w[0, 0], up_w[0, 0], down_w[0, 0]
    packed = jax.ShapeDtypeStruct((owners, height, LANES), BF16)
    spare = [pltpu.VMEM((owners * height, LANES), F32)]

    send, take = pl.pallas_call(
        functools.partial(tables_kernel, owners),
        out_shape=(
            jax.ShapeDtypeStruct((batches, tokens, SLOTS * owners), BF16),
            jax.ShapeDtypeStruct((batches, 2 * tokens, SLOTS * owners), BF16),
        ),
        in_specs=[vmem()] * 2,
        out_specs=(vmem(), vmem()),
        name="tables",
    )(route_ids[0], route_probs[0])
    held = jnp.clip(jnp.arange(steps, dtype=jnp.int32) - section, 0, batches - 1)

    layer_out = [jnp.zeros((tokens, feature), F32)] * batches
    hiddens = [jnp.zeros((SLOTS * owners, hidden_width), BF16)] * batches
    arrived = acts[0]
    for step in range(steps):
        if 0 < step < batches:
            arrived = jnp.where(section == 0, acts[step], arrived)
        outgoing = pl.pallas_call(
            functools.partial(dispatch_kernel, step, owners),
            out_shape=packed,
            in_specs=[smem()] + [vmem()] * 3,
            out_specs=vmem(),
            scratch_shapes=spare,
            name="dispatch",
        )(held, arrived, norm_gain, send)
        incoming = lax.all_to_all(outgoing, "expert", split_axis=0, concat_axis=0, tiled=True)
        output, hidden = pl.pallas_call(
            expert_kernel,
            out_shape=(packed, jax.ShapeDtypeStruct((SLOTS * owners, hidden_width), BF16)),
            in_specs=[vmem()] * 4,
            out_specs=(vmem(), vmem()),
            scratch_shapes=spare,
            name="expert",
        )(incoming, w_gate, w_up, w_down)
        back = lax.all_to_all(output, "expert", split_axis=0, concat_axis=0, tiled=True)
        result, sent = pl.pallas_call(
            functools.partial(combine_kernel, step),
            out_shape=(
                jax.ShapeDtypeStruct((tokens, feature), F32),
                jax.ShapeDtypeStruct((tokens, feature), BF16),
            ),
            in_specs=[smem()] + [vmem()] * 3,
            out_specs=(vmem(), vmem()),
            scratch_shapes=spare,
            name="combine",
        )(held, arrived, back, take)
        for batch in range(batches):
            own = step - section == batch
            layer_out[batch] = jnp.where(own, result, layer_out[batch])
            hiddens[batch] = jnp.where(own, hidden, hiddens[batch])
        if step < steps - 1:
            pairs = [
                (step - batch, step - batch + 1)
                for batch in range(batches)
                if 0 <= step - batch < sections - 1
            ]
            arrived = lax.ppermute(sent, "section", pairs)
    rows = jnp.concatenate(hiddens, axis=0)
    square = lax.dot_general(rows, rows, (((0,), (0,)), ((), ())), preferred_element_type=F32)
    return (jnp.stack(layer_out)[None], (scale * square)[None, None])


def solution(mesh):
    placed = (
        P(None, "expert", None),
        P("section", None),
        P("section", "expert", None, None),
        P("section", "expert", None, None),
        P("section", "expert", None, None),
        P("section", None, "expert", None),
        P("section", None, "expert", None),
    )
    return jax.shard_map(
        body,
        mesh=mesh,
        in_specs=placed,
        out_specs=(P("section", None, "expert", None), P("section", "expert", None, None)),
        check_vma=False,
    )
```

time: 745 us -> 731 us (0.981)
  the two profiles are of different devices: /device:TPU:16 before, /device:TPU:31 now
where the time goes in v1:
time: 731 us; the launch traced here: 718 us
  blocking collectives  419 us (57%)
  Pallas kernels  170 us (23%)
  waiting for transfers between devices  87.6 us (12%)
  starting transfers between devices  19.1 us (3%)
  local copies, waits for them, and re-layouts  14.6 us (2%)
    all_to_all x16, blocking collectives, body(): lax.all_to_all(outgoing, 'expert', split_axis=0, concat_axis=0, tiled=True)  217 us
    all_to_all x16, blocking collectives, body(): lax.all_to_all(output, 'expert', split_axis=0, concat_axis=0, tiled=True)  201 us
    pallas_call x17, Pallas kernels, body(): pl.pallas_call(expert_kernel, out_shape=(packed, jax.ShapeDtypeStruct((SL...  106 us
    ppermute x16, waiting for transfers between devices, body(): arrived = lax.ppermute(sent, 'section', pairs)  73.2 us
    pallas_call x17, Pallas kernels, body(): pl.pallas_call(functools.partial(dispatch_kernel, step, owners), out_shap...  31.2 us
    pallas_call x17, Pallas kernels, body(): pl.pallas_call(functools.partial(combine_kernel, step), out_shape=(jax.Sh...  31 us
  transfers between devices with their start and end apart: 18, of which 4 were waited for; matrix products, arithmetic and copies ran while one was open for 0% of the time, Pallas kernels for 0%

profile of v1, /device:TPU:31, one launch (start us, length us, event | category | flops | bytes accessed | tf_op | source)
XLA Modules:
  0.0 717.6 jit_solution(16651638445099755886)
XLA Ops:
  8.7 18.4 %all_to_all.170.in_ref = bf16[16,32,128]{2,1,0:T(8,128)(2,1)} all-to-all(bf16[16,32,128]{2,1,0:T(8,128)(2,1)} %dispatch.17), channel_id=1, replica_groups=mesh['section'=16,'expert'=16] {'expert'}, dimensions={0} | all-to-all | bytes 262144 | tf_op jit(solution)/shard_map/all_to_all | solution.py:148
  51.0 13.2 %all_to_all.172.in_ref = bf16[16,32,128]{2,1,0:T(8,128)(2,1)} all-to-all(bf16[16,32,128]{2,1,0:T(8,128)(2,1)} %dispatch.18), channel_id=1, replica_groups=mesh['section'=16,'expert'=16] {'expert'}, dimensions={0} | all-to-all | bytes 262144 | tf_op jit(solution)/shard_map/all_to_all | solution.py:148
  70.4 12.6 %all_to_all.173.back_ref = bf16[16,32,128]{2,1,0:T(8,128)(2,1)} all-to-all(bf16[16,32,128]{2,1,0:T(8,128)(2,1)} %get-tuple-element.75), channel_id=1, replica_groups=mesh['section'=16,'expert'=16] {'expert'}, dimensions={0} | all-to-all | bytes 262144 | tf_op jit(solution)/shard_map/all_to_all | solution.py:157
  87.9 13.2 %all_to_all.174.in_ref = bf16[16,32,128]{2,1,0:T(8,128)(2,1)} all-to-all(bf16[16,32,128]{2,1,0:T(8,128)(2,1)} %dispatch.19), channel_id=1, replica_groups=mesh['section'=16,'expert'=16] {'expert'}, dimensions={0} | all-to-all | bytes 262144 | tf_op jit(solution)/shard_map/all_to_all | solution.py:148
  107.3 12.6 %all_to_all.175.back_ref = bf16[16,32,128]{2,1,0:T(8,128)(2,1)} all-to-all(bf16[16,32,128]{2,1,0:T(8,128)(2,1)} %get-tuple-element.77), channel_id=1, replica_groups=mesh['section'=16,'expert'=16] {'expert'}, dimensions={0} | all-to-all | bytes 262144 | tf_op jit(solution)/shard_map/all_to_all | solution.py:157
  124.8 13.2 %all_to_all.176.in_ref = bf16[16,32,128]{2,1,0:T(8,128)(2,1)} all-to-all(bf16[16,32,128]{2,1,0:T(8,128)(2,1)} %dispatch.20), channel_id=1, replica_groups=mesh['section'=16,'expert'=16] {'expert'}, dimensions={0} | all-to-all | bytes 262144 | tf_op jit(solution)/shard_map/all_to_all | solution.py:148
  144.3 12.6 %all_to_all.177.back_ref = bf16[16,32,128]{2,1,0:T(8,128)(2,1)} all-to-all(bf16[16,32,128]{2,1,0:T(8,128)(2,1)} %get-tuple-element.79), channel_id=1, replica_groups=mesh['section'=16,'expert'=16] {'expert'}, dimensions={0} | all-to-all | bytes 262144 | tf_op jit(solution)/shard_map/all_to_all | solution.py:157
  161.8 13.2 %all_to_all.178.in_ref = bf16[16,32,128]{2,1,0:T(8,128)(2,1)} all-to-all(bf16[16,32,128]{2,1,0:T(8,128)(2,1)} %dispatch.21), channel_id=1, replica_groups=mesh['section'=16,'expert'=16] {'expert'}, dimensions={0} | all-to-all | bytes 262144 | tf_op jit(solution)/shard_map/all_to_all | solution.py:148
  181.2 12.6 %all_to_all.179.back_ref = bf16[16,32,128]{2,1,0:T(8,128)(2,1)} all-to-all(bf16[16,32,128]{2,1,0:T(8,128)(2,1)} %get-tuple-element.81), channel_id=1, replica_groups=mesh['section'=16,'expert'=16] {'expert'}, dimensions={0} | all-to-all | bytes 262144 | tf_op jit(solution)/shard_map/all_to_all | solution.py:157
  198.7 13.3 %all_to_all.180.in_ref = bf16[16,32,128]{2,1,0:T(8,128)(2,1)} all-to-all(bf16[16,32,128]{2,1,0:T(8,128)(2,1)} %dispatch.22), channel_id=1, replica_groups=mesh['section'=16,'expert'=16] {'expert'}, dimensions={0} | all-to-all | bytes 262144 | tf_op jit(solution)/shard_map/all_to_all | solution.py:148
  235.8 13.2 %all_to_all.182.in_ref = bf16[16,32,128]{2,1,0:T(8,128)(2,1)} all-to-all(bf16[16,32,128]{2,1,0:T(8,128)(2,1)} %dispatch.23), channel_id=1, replica_groups=mesh['section'=16,'expert'=16] {'expert'}, dimensions={0} | all-to-all | bytes 262144 | tf_op jit(solution)/shard_map/all_to_all | solution.py:148
  255.2 12.6 %all_to_all.183.back_ref = bf16[16,32,128]{2,1,0:T(8,128)(2,1)} all-to-all(bf16[16,32,128]{2,1,0:T(8,128)(2,1)} %get-tuple-element.85), channel_id=1, replica_groups=mesh['section'=16,'expert'=16] {'expert'}, dimensions={0} | all-to-all | bytes 262144 | tf_op jit(solution)/shard_map/all_to_all | solution.py:157
  272.8 13.2 %all_to_all.184.in_ref = bf16[16,32,128]{2,1,0:T(8,128)(2,1)} all-to-all(bf16[16,32,128]{2,1,0:T(8,128)(2,1)} %dispatch.24), channel_id=1, replica_groups=mesh['section'=16,'expert'=16] {'expert'}, dimensions={0} | all-to-all | bytes 262144 | tf_op jit(solution)/shard_map/all_to_all | solution.py:148
  309.7 13.2 %all_to_all.186.in_ref = bf16[16,32,128]{2,1,0:T(8,128)(2,1)} all-to-all(bf16[16,32,128]{2,1,0:T(8,128)(2,1)} %dispatch.25), channel_id=1, replica_groups=mesh['section'=16,'expert'=16] {'expert'}, dimensions={0} | all-to-all | bytes 262144 | tf_op jit(solution)/shard_map/all_to_all | solution.py:148
  329.1 12.6 %all_to_all.187.back_ref = bf16[16,32,128]{2,1,0:T(8,128)(2,1)} all-to-all(bf16[16,32,128]{2,1,0:T(8,128)(2,1)} %get-tuple-element.89), channel_id=1, replica_groups=mesh['section'=16,'expert'=16] {'expert'}, dimensions={0} | all-to-all | bytes 262144 | tf_op jit(solution)/shard_map/all_to_all | solution.py:157
  346.6 13.2 %all_to_all.188.in_ref = bf16[16,32,128]{2,1,0:T(8,128)(2,1)} all-to-all(bf16[16,32,128]{2,1,0:T(8,128)(2,1)} %dispatch.26), channel_id=1, replica_groups=mesh['section'=16,'expert'=16] {'expert'}, dimensions={0} | all-to-all | bytes 262144 | tf_op jit(solution)/shard_map/all_to_all | solution.py:148
  383.6 13.4 %all_to_all.190.in_ref = bf16[16,32,128]{2,1,0:T(8,128)(2,1)} all-to-all(bf16[16,32,128]{2,1,0:T(8,128)(2,1)} %dispatch.27), channel_id=1, replica_groups=mesh['section'=16,'expert'=16] {'expert'}, dimensions={0} | all-to-all | bytes 262144 | tf_op jit(solution)/shard_map/all_to_all | solution.py:148
  420.7 13.2 %all_to_all.192.in_ref = bf16[16,32,128]{2,1,0:T(8,128)(2,1)} all-to-all(bf16[16,32,128]{2,1,0:T(8,128)(2,1)} %dispatch.28), channel_id=1, replica_groups=mesh['section'=16,'expert'=16] {'expert'}, dimensions={0} | all-to-all | bytes 262144 | tf_op jit(solution)/shard_map/all_to_all | solution.py:148
  457.6 13.2 %all_to_all.194.in_ref = bf16[16,32,128]{2,1,0:T(8,128)(2,1)} all-to-all(bf16[16,32,128]{2,1,0:T(8,128)(2,1)} %dispatch.29), channel_id=1, replica_groups=mesh['section'=16,'expert'=16] {'expert'}, dimensions={0} | all-to-all | bytes 262144 | tf_op jit(solution)/shard_map/all_to_all | solution.py:148
  494.6 13.2 %all_to_all.196.in_ref = bf16[16,32,128]{2,1,0:T(8,128)(2,1)} all-to-all(bf16[16,32,128]{2,1,0:T(8,128)(2,1)} %dispatch.30), channel_id=1, replica_groups=mesh['section'=16,'expert'=16] {'expert'}, dimensions={0} | all-to-all | bytes 262144 | tf_op jit(solution)/shard_map/all_to_all | solution.py:148
  531.5 13.2 %all_to_all.198.in_ref = bf16[16,32,128]{2,1,0:T(8,128)(2,1)} all-to-all(bf16[16,32,128]{2,1,0:T(8,128)(2,1)} %dispatch.31), channel_id=1, replica_groups=mesh['section'=16,'expert'=16] {'expert'}, dimensions={0} | all-to-all | bytes 262144 | tf_op jit(solution)/shard_map/all_to_all | solution.py:148
  566.6 68.7 %collective-permute-done.14.x_ref = bf16[8,2048]{1,0:T(8,128)(2,1)S(1)} collective-permute-done((bf16[8,2048]{1,0:T(8,128)(2,1)}, bf16[8,2048]{1,0:T(8,128)(2,1)S(1)}, u32[]{:S(2)}, u32[]{:S(2)}) %collective-permute-start.14) | collective-permute-done | bytes 32800 | tf_op jit(solution)/shard_map/ppermute | solution.py:179
  637.8 14.0 %all_to_all.200.in_ref = bf16[16,32,128]{2,1,0:T(8,128)(2,1)} all-to-all(bf16[16,32,128]{2,1,0:T(8,128)(2,1)} %dispatch.32), channel_id=1, replica_groups=mesh['section'=16,'expert'=16] {'expert'}, dimensions={0} | all-to-all | bytes 262144 | tf_op jit(solution)/shard_map/all_to_all | solution.py:148
  658.0 12.6 %all_to_all.201.back_ref = bf16[16,32,128]{2,1,0:T(8,128)(2,1)} all-to-all(bf16[16,32,128]{2,1,0:T(8,128)(2,1)} %get-tuple-element.103), channel_id=1, replica_groups=mesh['section'=16,'expert'=16] {'expert'}, dimensions={0} | all-to-all | bytes 262144 | tf_op jit(solution)/shard_map/all_to_all | solution.py:157
  (207 shorter events, 341.5 us)
Async XLA Ops:
  27.1 21.3 %copy-start.49 = (bf16[2,8,2048]{2,1,0:T(8,128)(2,1)S(1)}, bf16[2,8,2048]{2,1,0:T(8,128)(2,1)}, u32[]{:S(2)}) copy-start(bf16[2,8,2048]{2,1,0:T(8,128)(2,1)} %param.7) | copy-start | bytes 196612
  47.8 0.7 collective-permute-start
  84.8 0.7 collective-permute-start.1
  121.7 0.7 collective-permute-start.2
  158.7 0.7 collective-permute-start.3
  195.6 0.7 collective-permute-start.4
  232.7 0.7 collective-permute-start.5
  269.6 0.7 collective-permute-start.6
  306.6 0.7 collective-permute-start.7
  343.5 0.7 collective-permute-start.8
  380.5 0.7 collective-permute-start.9
  417.6 0.7 collective-permute-start.10
  454.5 0.7 collective-permute-start.11
  491.5 0.7 collective-permute-start.12
  528.4 0.7 collective-permute-start.13
  565.4 70.0 %collective-permute-start.14 = (bf16[8,2048]{1,0:T(8,128)(2,1)}, bf16[8,2048]{1,0:T(8,128)(2,1)S(1)}, u32[]{:S(2)}, u32[]{:S(2)}) collective-permute-start(bf16[8,2048]{1,0:T(8,128)(2,1)} %get-tuple-element.102), channel_id=1, source_target_pairs={{224,240},{208,224},{225,241},{209,225},{226,242},{210,226},{227,2... | collective-permute-start | bytes 98312 | tf_op jit(solution)/shard_map/ppermute | solution.py:179
  672.5 5.7 collective-permute-start.15
  680.6 13.1 %all-to-all-start.32 = ((bf16[16,32,128]{2,1,0:T(8,128)(2,1)}), bf16[16,32,128]{2,1,0:T(8,128)(2,1)S(1)}, u32[]{:S(2)}, u32[]{:S(2)}) async-start(bf16[16,32,128]{2,1,0:T(8,128)(2,1)} %dispatch.33), calls=%async_computation.32 | async-start | bytes 262144 | tf_op jit(solution)/shard_map/all_to_all | solution.py:148
  684.5 19.8 %copy-start.19 = (bf16[32,768]{1,0:T(8,128)(2,1)S(1)}, bf16[32,768]{1,0:T(8,128)(2,1)}, u32[]{:S(2)}) copy-start(bf16[32,768]{1,0:T(8,128)(2,1)} %get-tuple-element.138) | copy-start | bytes 147460
  684.5 19.8 %copy-start.20 = (bf16[32,768]{1,0:T(8,128)(2,1)S(1)}, bf16[32,768]{1,0:T(8,128)(2,1)}, u32[]{:S(2)}) copy-start(bf16[32,768]{1,0:T(8,128)(2,1)} %get-tuple-element.137) | copy-start | bytes 147460
  684.5 19.8 %copy-start.21 = (bf16[32,768]{1,0:T(8,128)(2,1)S(1)}, bf16[32,768]{1,0:T(8,128)(2,1)}, u32[]{:S(2)}) copy-start(bf16[32,768]{1,0:T(8,128)(2,1)} %get-tuple-element.136) | copy-start | bytes 147460
  684.5 19.8 %copy-start.22 = (bf16[32,768]{1,0:T(8,128)(2,1)S(1)}, bf16[32,768]{1,0:T(8,128)(2,1)}, u32[]{:S(2)}) copy-start(bf16[32,768]{1,0:T(8,128)(2,1)} %get-tuple-element.135) | copy-start | bytes 147460
  684.5 19.8 %copy-start.23 = (bf16[32,768]{1,0:T(8,128)(2,1)S(1)}, bf16[32,768]{1,0:T(8,128)(2,1)}, u32[]{:S(2)}) copy-start(bf16[32,768]{1,0:T(8,128)(2,1)} %get-tuple-element.134) | copy-start | bytes 147460
  700.7 12.1 %all-to-all-start.33 = ((bf16[16,32,128]{2,1,0:T(8,128)(2,1)}), bf16[16,32,128]{2,1,0:T(8,128)(2,1)S(1)}, u32[]{:S(2)}, u32[]{:S(2)}) async-start(bf16[16,32,128]{2,1,0:T(8,128)(2,1)} %get-tuple-element.105), calls=%async_computation.33 | async-start | bytes 262144 | tf_op jit(solution)/shard_map/all_to_all | solution.py:157
  (44 other events, 463.5 us)

commit v2 on v1

v2 whole, which is shorter than its diff:
```python
import functools

import jax
import jax.numpy as jnp
from jax import lax
from jax.experimental import pallas as pl
from jax.experimental.pallas import tpu as pltpu
from jax.sharding import PartitionSpec as P

LANES = 128
SLOTS = 2
BF16 = jnp.bfloat16
F32 = jnp.float32


MIB = 1 << 20


def params(mib):
    return pltpu.CompilerParams(vmem_limit_bytes=mib * MIB)


def vmem():
    return pl.BlockSpec(memory_space=pltpu.VMEM)


def spread_rows(rows, spare, owners):
    blocks = rows.shape[1] // LANES
    for slot in range(SLOTS):
        for block in range(blocks):
            spare[pl.ds(slot * blocks + block, owners, stride=SLOTS * blocks), :] = rows[
                slot * owners : (slot + 1) * owners, block * LANES : (block + 1) * LANES
            ]


def gather_rows(spare, owners, blocks):
    parts = []
    for slot in range(SLOTS):
        parts.append(
            jnp.concatenate(
                [
                    spare[pl.ds(slot * blocks + block, owners, stride=SLOTS * blocks), :]
                    for block in range(blocks)
                ],
                axis=1,
            )
        )
    return jnp.concatenate(parts, axis=0)


def weights_kernel(*refs):
    hidden_ref = refs[-1]
    hidden_ref[...] = jnp.zeros_like(hidden_ref)


def tables_kernel(owners, ids_ref, probs_ref, send_ref, take_ref, layer_ref):
    layer_ref[...] = jnp.zeros_like(layer_ref)
    batches, picks, tokens = ids_ref.shape
    experts = lax.broadcasted_iota(jnp.int32, (owners, tokens), 0)
    earlier = (
        lax.broadcasted_iota(jnp.int32, (tokens, tokens), 0)
        < lax.broadcasted_iota(jnp.int32, (tokens, tokens), 1)
    ).astype(BF16)
    for batch in range(batches):
        ids = ids_ref[batch]
        probs = probs_ref[batch]
        named = jnp.zeros((owners, tokens), F32)
        weight = jnp.zeros((owners, tokens), F32)
        for pick in range(picks):
            hit = ids[pick : pick + 1, :] == experts
            named = named + jnp.where(hit, 1.0, 0.0)
            weight = weight + jnp.where(hit, probs[pick : pick + 1, :], 0.0)
        slot = jnp.dot(named.astype(BF16), earlier, preferred_element_type=F32)
        split = [jnp.abs(slot - number) < 0.5 for number in range(SLOTS)]
        send = jnp.concatenate([jnp.where(own, named, 0.0) for own in split], axis=0)
        take = jnp.concatenate([jnp.where(own, weight, 0.0) for own in split], axis=0)
        send_ref[batch] = send.astype(BF16)
        high = take.astype(BF16).astype(F32)
        take_ref[batch] = jnp.concatenate([high, take - high], axis=1).astype(BF16)


def when_active(step, batches):
    batch = step - lax.axis_index("section")

    def call(function):
        pl.when((batch >= 0) & (batch < batches))(lambda: function(batch))

    return call


def dispatch_kernel(step, owners, batches, *refs):
    *sources, gain_ref, send_ref, out_ref, x_ref, spare = refs

    @when_active(step, batches)
    def _(held):
        if step == 0:
            x = sources[0][0]
        elif step < batches:
            x = jnp.where(held == step, sources[1][step], sources[0][...])
        else:
            x = sources[0][...]
        x_ref[...] = x
        wide = x.astype(F32)
        mean = jnp.mean(wide * wide, axis=-1, keepdims=True)
        normed = (wide * lax.rsqrt(mean + 1e-06) * gain_ref[...]).astype(BF16)
        rows = jnp.dot(send_ref[held], normed, preferred_element_type=F32)
        spread_rows(rows, spare, owners)
        out_ref[...] = spare[...].astype(BF16).reshape(out_ref.shape)


def expert_kernel(step, batches, in_ref, gate_ref, up_ref, down_ref, _, out_ref, hidden_ref, spare):
    owners, height, lanes = in_ref.shape

    @when_active(step, batches)
    def _(held):
        spare[...] = in_ref[...].astype(F32).reshape(owners * height, lanes)
        rows = gather_rows(spare, owners, height // SLOTS).astype(BF16)
        gate = jnp.dot(rows, gate_ref[...], preferred_element_type=F32)
        upper = jnp.dot(rows, up_ref[...], preferred_element_type=F32)
        hidden = (gate / (1.0 + jnp.exp(-gate)) * upper).astype(BF16)
        hidden_ref[held] = hidden
        output = jnp.dot(hidden, down_ref[...], preferred_element_type=F32)
        spread_rows(output, spare, owners)
        out_ref[...] = spare[...].astype(BF16).reshape(out_ref.shape)


def combine_kernel(
    step, batches, last, x_ref, back_ref, take_ref, before_ref, sent_ref, out_ref, spare
):
    owners, height, lanes = back_ref.shape
    tokens = x_ref.shape[0]
    if last:
        out_ref[...] = before_ref[...]

    @when_active(step, batches)
    def _(held):
        spare[...] = back_ref[...].astype(F32).reshape(owners * height, lanes)
        rows = gather_rows(spare, owners, height // SLOTS).astype(BF16)
        mixed = lax.dot_general(
            take_ref[held], rows, (((0,), (0,)), ((), ())), preferred_element_type=F32
        )
        result = x_ref[...].astype(F32) + (mixed[:tokens] + mixed[tokens:])
        sent_ref[...] = result.astype(BF16)
        out_ref[held] = result


def onward(step, batches, sections):
    row = 4 if sections % 4 == 0 else sections
    needed = [step - batch for batch in range(batches) if 0 <= step - batch < sections - 1]
    if step % row < row - 2:
        return [(place, place + 1) for place in needed]
    if any((place + 1) % row == 0 for place in needed):
        row = sections
    return [(place, place - place % row + (place + 1) % row) for place in range(sections)]


def body(acts, norm_gain, gate_w, up_w, down_w, route_ids, route_probs):
    sections = lax.axis_size("section")
    owners = lax.axis_size("expert")
    batches, tokens, feature = acts.shape
    picks = route_ids.shape[-1]
    hidden_width = gate_w.shape[-1]
    steps = batches + sections - 1
    height = SLOTS * feature // LANES
    scale = 2.0 / (batches * tokens * picks)
    w_gate, w_up, w_down = gate_w[0, 0], up_w[0, 0], down_w[0, 0]
    packed = jax.ShapeDtypeStruct((owners, height, LANES), BF16)
    held_x = jax.ShapeDtypeStruct((tokens, feature), BF16)
    hidden_shape = jax.ShapeDtypeStruct((batches, SLOTS * owners, hidden_width), BF16)
    layer_shape = jax.ShapeDtypeStruct((batches, tokens, feature), F32)
    spare = [pltpu.VMEM((owners * height, LANES), F32)]

    hiddens = pl.pallas_call(
        weights_kernel,
        out_shape=hidden_shape,
        in_specs=[vmem()] * 3,
        out_specs=vmem(),
        compiler_params=params(2),
        cost_estimate=pl.CostEstimate(
            flops=0, bytes_accessed=4 * 3 * w_gate.size, transcendentals=0
        ),
        name="weights",
    )(w_gate, w_up, w_down)
    send, take, layer_out = pl.pallas_call(
        functools.partial(tables_kernel, owners),
        out_shape=(
            jax.ShapeDtypeStruct((batches, SLOTS * owners, tokens), BF16),
            jax.ShapeDtypeStruct((batches, SLOTS * owners, 2 * tokens), BF16),
            layer_shape,
        ),
        in_specs=[vmem()] * 2,
        out_specs=(vmem(),) * 3,
        compiler_params=params(2),
        name="tables",
    )(jnp.swapaxes(route_ids[0], 1, 2), jnp.swapaxes(route_probs[0], 1, 2))

    sources = [acts]
    for step in range(steps):
        last = step == steps - 1
        outgoing, wide = pl.pallas_call(
            functools.partial(dispatch_kernel, step, owners, batches),
            out_shape=(packed, held_x),
            in_specs=[vmem()] * (len(sources) + 2),
            out_specs=(vmem(), vmem()),
            scratch_shapes=spare,
            compiler_params=params(2),
            name="dispatch",
        )(*sources, norm_gain, send)
        incoming = lax.all_to_all(outgoing, "expert", split_axis=0, concat_axis=0, tiled=True)
        output, hiddens = pl.pallas_call(
            functools.partial(expert_kernel, step, batches),
            out_shape=(packed, hidden_shape),
            in_specs=[vmem()] * 5,
            out_specs=(vmem(), vmem()),
            scratch_shapes=spare,
            input_output_aliases={4: 1},
            compiler_params=params(2),
            name="expert",
        )(incoming, w_gate, w_up, w_down, hiddens)
        back = lax.all_to_all(output, "expert", split_axis=0, concat_axis=0, tiled=True)
        sent, layer_out = pl.pallas_call(
            functools.partial(combine_kernel, step, batches, last),
            out_shape=(held_x, layer_shape),
            in_specs=[vmem()] * 4,
            out_specs=(vmem(), vmem()),
            scratch_shapes=spare,
            input_output_aliases={} if last else {3: 1},
            compiler_params=params(2),
            name="combine",
        )(wide, back, take, layer_out)
        if not last:
            arrived = lax.ppermute(sent, "section", onward(step, batches, sections))
            sources = [arrived, acts] if step + 1 < batches else [arrived]
    rows = hiddens.reshape(batches * SLOTS * owners, hidden_width)
    square = lax.dot_general(rows, rows, (((0,), (0,)), ((), ())), preferred_element_type=F32)
    return (layer_out[None], (scale * square)[None, None])


def solution(mesh):
    placed = (
        P(None, "expert", None),
        P("section", None),
        P("section", "expert", None, None),
        P("section", "expert", None, None),
        P("section", "expert", None, None),
        P("section", None, "expert", None),
        P("section", None, "expert", None),
    )
    return jax.shard_map(
        body,
        mesh=mesh,
        in_specs=placed,
        out_specs=(P("section", None, "expert", None), P("section", "expert", None, None)),
        check_vma=False,
    )
```

time: 731 us -> 532 us (0.73)
  Pallas kernels: 170 us -> 8 us
  starting transfers between devices: 19.1 us -> 89.1 us
  waiting for transfers between devices: 87.6 us -> 29.2 us
  blocking collectives: 419 us -> 379 us
    pallas_call x51 -> x52, Pallas kernels: 168 us -> 7.79 us  [the longest x17 5 us: body(): pl.pallas_call(functools.partial(expert_kernel, step, batches), out_shape...]
    ppermute x16, starting transfers between devices: 11.7 us -> 76.6 us  [body(): arrived = lax.ppermute(sent, 'section', onward(step, batches, sections))]
    ppermute x16, waiting for transfers between devices: 73.2 us -> 19.2 us  [body(): arrived = lax.ppermute(sent, 'section', onward(step, batches, sections))]
    all_to_all x16, blocking collectives: 217 us -> 191 us  [body(): lax.all_to_all(outgoing, 'expert', split_axis=0, concat_axis=0, tiled=True)]
    all_to_all x16, blocking collectives: 201 us -> 189 us  [body(): lax.all_to_all(output, 'expert', split_axis=0, concat_axis=0, tiled=True)]
  transfers between devices with their start and end apart: 18 -> 18, of which waited for: 4 -> 10; matrix products, arithmetic and copies ran while one was open for 0% -> 0% of each run, Pallas kernels for 0% -> 0%
where the time goes in v2:
time: 532 us; the launch traced here: 522 us
  blocking collectives  379 us (71%)
  starting transfers between devices  89.1 us (17%)
  waiting for transfers between devices  29.2 us (5%)
  local copies, waits for them, and re-layouts  13 us (2%)
  Pallas kernels  8 us (2%)
    all_to_all x16, blocking collectives, body(): lax.all_to_all(outgoing, 'expert', split_axis=0, concat_axis=0, tiled=True)  191 us
    all_to_all x16, blocking collectives, body(): lax.all_to_all(output, 'expert', split_axis=0, concat_axis=0, tiled=True)  189 us
    ppermute x16, starting transfers between devices, body(): arrived = lax.ppermute(sent, 'section', onward(step, batches, sections))  76.6 us
    ppermute x16, waiting for transfers between devices, body(): arrived = lax.ppermute(sent, 'section', onward(step, batches, sections))  19.2 us
    unnamed x30, local copies, waits for them, and re-layouts  13 us
  transfers between devices with their start and end apart: 18, of which 10 were waited for; matrix products, arithmetic and copies ran while one was open for 0% of the time, Pallas kernels for 0%

profile of v2, /device:TPU:31, one launch (start us, length us, event | category | flops | bytes accessed | tf_op | source)
XLA Modules:
  0.0 521.6 jit_solution(596125513848907603)
XLA Ops:
  27.1 14.8 %all_to_all.170.back_ref = bf16[16,32,128]{2,1,0:T(8,128)(2,1)S(1)} all-to-all(bf16[16,32,128]{2,1,0:T(8,128)(2,1)S(1)} %get-tuple-element.109), channel_id=1, replica_groups=mesh['section'=16,'expert'=16] {'expert'}, dimensions={0} | all-to-all | bytes 262144 | tf_op jit(solution)/shard_map/all_to_all | solution.py:220
  42.7 11.6 %all_to_all.171.in_ref = bf16[16,32,128]{2,1,0:T(8,128)(2,1)S(1)} all-to-all(bf16[16,32,128]{2,1,0:T(8,128)(2,1)S(1)} %get-tuple-element.114), channel_id=1, replica_groups=mesh['section'=16,'expert'=16] {'expert'}, dimensions={0} | all-to-all | bytes 262144 | tf_op jit(solution)/shard_map/all_to_all | solution.py:209
  54.3 11.6 %all_to_all.172.back_ref = bf16[16,32,128]{2,1,0:T(8,128)(2,1)S(1)} all-to-all(bf16[16,32,128]{2,1,0:T(8,128)(2,1)S(1)} %get-tuple-element.116), channel_id=1, replica_groups=mesh['section'=16,'expert'=16] {'expert'}, dimensions={0} | all-to-all | bytes 262144 | tf_op jit(solution)/shard_map/all_to_all | solution.py:220
  66.6 11.6 %all_to_all.173.in_ref = bf16[16,32,128]{2,1,0:T(8,128)(2,1)S(1)} all-to-all(bf16[16,32,128]{2,1,0:T(8,128)(2,1)S(1)} %get-tuple-element.120), channel_id=1, replica_groups=mesh['section'=16,'expert'=16] {'expert'}, dimensions={0} | all-to-all | bytes 262144 | tf_op jit(solution)/shard_map/all_to_all | solution.py:209
  93.0 12.2 %all_to_all.175.in_ref = bf16[16,32,128]{2,1,0:T(8,128)(2,1)S(1)} all-to-all(bf16[16,32,128]{2,1,0:T(8,128)(2,1)S(1)} %get-tuple-element.126), channel_id=1, replica_groups=mesh['section'=16,'expert'=16] {'expert'}, dimensions={0} | all-to-all | bytes 262144 | tf_op jit(solution)/shard_map/all_to_all | solution.py:209
  116.8 14.3 %collective-permute-start.3 = (bf16[8,2048]{1,0:T(8,128)(2,1)S(1)}, bf16[8,2048]{1,0:T(8,128)(2,1)S(1)}, u32[]{:S(2)}, u32[]{:S(2)}) collective-permute-start(bf16[8,2048]{1,0:T(8,128)(2,1)S(1)} %get-tuple-element.130), channel_id=1, source_target_pairs={{0,16},{16,32},{32,48},{48,64},{64,80},{80,96},{96,112},{112,128},... | collective-permute-start | bytes 98312 | tf_op jit(solution)/shard_map/ppermute | solution.py:232
  132.2 12.4 %all_to_all.177.in_ref = bf16[16,32,128]{2,1,0:T(8,128)(2,1)S(1)} all-to-all(bf16[16,32,128]{2,1,0:T(8,128)(2,1)S(1)} %get-tuple-element.132), channel_id=1, replica_groups=mesh['section'=16,'expert'=16] {'expert'}, dimensions={0} | all-to-all | bytes 262144 | tf_op jit(solution)/shard_map/all_to_all | solution.py:209
  144.8 11.6 %all_to_all.178.back_ref = bf16[16,32,128]{2,1,0:T(8,128)(2,1)S(1)} all-to-all(bf16[16,32,128]{2,1,0:T(8,128)(2,1)S(1)} %get-tuple-element.134), channel_id=1, replica_groups=mesh['section'=16,'expert'=16] {'expert'}, dimensions={0} | all-to-all | bytes 262144 | tf_op jit(solution)/shard_map/all_to_all | solution.py:220
  157.1 11.6 %all_to_all.179.in_ref = bf16[16,32,128]{2,1,0:T(8,128)(2,1)S(1)} all-to-all(bf16[16,32,128]{2,1,0:T(8,128)(2,1)S(1)} %get-tuple-element.138), channel_id=1, replica_groups=mesh['section'=16,'expert'=16] {'expert'}, dimensions={0} | all-to-all | bytes 262144 | tf_op jit(solution)/shard_map/all_to_all | solution.py:209
  180.9 11.6 %all_to_all.181.in_ref = bf16[16,32,128]{2,1,0:T(8,128)(2,1)S(1)} all-to-all(bf16[16,32,128]{2,1,0:T(8,128)(2,1)S(1)} %get-tuple-element.144), channel_id=1, replica_groups=mesh['section'=16,'expert'=16] {'expert'}, dimensions={0} | all-to-all | bytes 262144 | tf_op jit(solution)/shard_map/all_to_all | solution.py:209
  207.4 12.2 %all_to_all.183.in_ref = bf16[16,32,128]{2,1,0:T(8,128)(2,1)S(1)} all-to-all(bf16[16,32,128]{2,1,0:T(8,128)(2,1)S(1)} %get-tuple-element.150), channel_id=1, replica_groups=mesh['section'=16,'expert'=16] {'expert'}, dimensions={0} | all-to-all | bytes 262144 | tf_op jit(solution)/shard_map/all_to_all | solution.py:209
  243.1 12.4 %all_to_all.185.in_ref = bf16[16,32,128]{2,1,0:T(8,128)(2,1)S(1)} all-to-all(bf16[16,32,128]{2,1,0:T(8,128)(2,1)S(1)} %get-tuple-element.156), channel_id=1, replica_groups=mesh['section'=16,'expert'=16] {'expert'}, dimensions={0} | all-to-all | bytes 262144 | tf_op jit(solution)/shard_map/all_to_all | solution.py:209
  255.9 11.6 %all_to_all.186.back_ref = bf16[16,32,128]{2,1,0:T(8,128)(2,1)S(1)} all-to-all(bf16[16,32,128]{2,1,0:T(8,128)(2,1)S(1)} %get-tuple-element.158), channel_id=1, replica_groups=mesh['section'=16,'expert'=16] {'expert'}, dimensions={0} | all-to-all | bytes 262144 | tf_op jit(solution)/shard_map/all_to_all | solution.py:220
  268.2 11.6 %all_to_all.187.in_ref = bf16[16,32,128]{2,1,0:T(8,128)(2,1)S(1)} all-to-all(bf16[16,32,128]{2,1,0:T(8,128)(2,1)S(1)} %get-tuple-element.162), channel_id=1, replica_groups=mesh['section'=16,'expert'=16] {'expert'}, dimensions={0} | all-to-all | bytes 262144 | tf_op jit(solution)/shard_map/all_to_all | solution.py:209
  292.0 11.6 %all_to_all.189.in_ref = bf16[16,32,128]{2,1,0:T(8,128)(2,1)S(1)} all-to-all(bf16[16,32,128]{2,1,0:T(8,128)(2,1)S(1)} %get-tuple-element.168), channel_id=1, replica_groups=mesh['section'=16,'expert'=16] {'expert'}, dimensions={0} | all-to-all | bytes 262144 | tf_op jit(solution)/shard_map/all_to_all | solution.py:209
  318.5 12.2 %all_to_all.191.in_ref = bf16[16,32,128]{2,1,0:T(8,128)(2,1)S(1)} all-to-all(bf16[16,32,128]{2,1,0:T(8,128)(2,1)S(1)} %get-tuple-element.174), channel_id=1, replica_groups=mesh['section'=16,'expert'=16] {'expert'}, dimensions={0} | all-to-all | bytes 262144 | tf_op jit(solution)/shard_map/all_to_all | solution.py:209
  354.7 12.4 %all_to_all.193.in_ref = bf16[16,32,128]{2,1,0:T(8,128)(2,1)S(1)} all-to-all(bf16[16,32,128]{2,1,0:T(8,128)(2,1)S(1)} %get-tuple-element.180), channel_id=1, replica_groups=mesh['section'=16,'expert'=16] {'expert'}, dimensions={0} | all-to-all | bytes 262144 | tf_op jit(solution)/shard_map/all_to_all | solution.py:209
  367.2 11.6 %all_to_all.194.back_ref = bf16[16,32,128]{2,1,0:T(8,128)(2,1)S(1)} all-to-all(bf16[16,32,128]{2,1,0:T(8,128)(2,1)S(1)} %get-tuple-element.182), channel_id=1, replica_groups=mesh['section'=16,'expert'=16] {'expert'}, dimensions={0} | all-to-all | bytes 262144 | tf_op jit(solution)/shard_map/all_to_all | solution.py:220
  379.5 11.6 %all_to_all.195.in_ref = bf16[16,32,128]{2,1,0:T(8,128)(2,1)S(1)} all-to-all(bf16[16,32,128]{2,1,0:T(8,128)(2,1)S(1)} %get-tuple-element.186), channel_id=1, replica_groups=mesh['section'=16,'expert'=16] {'expert'}, dimensions={0} | all-to-all | bytes 262144 | tf_op jit(solution)/shard_map/all_to_all | solution.py:209
  403.4 11.6 %all_to_all.197.in_ref = bf16[16,32,128]{2,1,0:T(8,128)(2,1)S(1)} all-to-all(bf16[16,32,128]{2,1,0:T(8,128)(2,1)S(1)} %get-tuple-element.192), channel_id=1, replica_groups=mesh['section'=16,'expert'=16] {'expert'}, dimensions={0} | all-to-all | bytes 262144 | tf_op jit(solution)/shard_map/all_to_all | solution.py:209
  426.5 33.6 %collective-permute-start.14 = (bf16[8,2048]{1,0:T(8,128)(2,1)S(1)}, bf16[8,2048]{1,0:T(8,128)(2,1)S(1)}, u32[]{:S(2)}, u32[]{:S(2)}) collective-permute-start(bf16[8,2048]{1,0:T(8,128)(2,1)S(1)} %get-tuple-element.196), channel_id=1, source_target_pairs={{0,16},{16,32},{32,48},{48,0},{64,80},{80,96},{96,112},{112,64},{1... | collective-permute-start | bytes 98312 | tf_op jit(solution)/shard_map/ppermute | solution.py:232
  463.0 12.1 %all_to_all.199.in_ref = bf16[16,32,128]{2,1,0:T(8,128)(2,1)S(1)} all-to-all(bf16[16,32,128]{2,1,0:T(8,128)(2,1)S(1)} %get-tuple-element.198), channel_id=1, replica_groups=mesh['section'=16,'expert'=16] {'expert'}, dimensions={0} | all-to-all | bytes 262144 | tf_op jit(solution)/shard_map/all_to_all | solution.py:209
  476.9 11.6 %all_to_all.200.back_ref = bf16[16,32,128]{2,1,0:T(8,128)(2,1)S(1)} all-to-all(bf16[16,32,128]{2,1,0:T(8,128)(2,1)S(1)} %get-tuple-element.200), channel_id=1, replica_groups=mesh['section'=16,'expert'=16] {'expert'}, dimensions={0} | all-to-all | bytes 262144 | tf_op jit(solution)/shard_map/all_to_all | solution.py:220
  494.1 12.1 %all_to_all.201.in_ref = bf16[16,32,128]{2,1,0:T(8,128)(2,1)S(1)} all-to-all(bf16[16,32,128]{2,1,0:T(8,128)(2,1)S(1)} %get-tuple-element.204), channel_id=1, replica_groups=mesh['section'=16,'expert'=16] {'expert'}, dimensions={0} | all-to-all | bytes 262144 | tf_op jit(solution)/shard_map/all_to_all | solution.py:209
  (128 shorter events, 209.1 us)
Async XLA Ops:
  5.0 18.3 %all-to-all-start = ((bf16[16,32,128]{2,1,0:T(8,128)(2,1)}), bf16[16,32,128]{2,1,0:T(8,128)(2,1)S(1)}, u32[]{:S(2)}, u32[]{:S(2)}) async-start(bf16[16,32,128]{2,1,0:T(8,128)(2,1)} %get-tuple-element.108), calls=%async_computation | async-start | bytes 262144 | tf_op jit(solution)/shard_map/all_to_all | solution.py:209
  19.8 3.5 copy-start.1
  23.3 1.9 copy-start.3
  27.1 14.9 %copy-start.12 = (bf16[8,2048]{1,0:T(8,128)(2,1)S(1)}, bf16[8,2048]{1,0:T(8,128)(2,1)}, u32[]{:S(2)}) copy-start(bf16[8,2048]{1,0:T(8,128)(2,1)} %copy-done.11) | copy-start | bytes 98308
  27.1 15.5 %copy-start.8 = (f32[1,2048]{1,0:T(1,128)S(1)}, f32[1,2048]{1,0:T(1,128)}, u32[]{:S(2)}) copy-start(f32[1,2048]{1,0:T(1,128)} %refs_1_.33) | copy-start | bytes 24580
  27.1 15.6 %copy-start.10 = (bf16[2,8,2048]{2,1,0:T(8,128)(2,1)S(1)}, bf16[2,8,2048]{2,1,0:T(8,128)(2,1)}, u32[]{:S(2)}) copy-start(bf16[2,8,2048]{2,1,0:T(8,128)(2,1)} %refs_1_.18) | copy-start | bytes 196612
  27.1 27.2 %copy-start.4 = (bf16[1,1,2048,768]{3,2,1,0:T(8,128)(2,1)S(1)}, bf16[1,1,2048,768]{3,2,1,0:T(8,128)(2,1)}, u32[]{:S(2)}) copy-start(bf16[1,1,2048,768]{3,2,1,0:T(8,128)(2,1)} %param.10) | copy-start | bytes 9437188
  42.0 0.7 collective-permute-start
  65.9 0.7 collective-permute-start.1
  89.7 3.3 collective-permute-start.2
  116.8 15.4 %collective-permute-start.3 = (bf16[8,2048]{1,0:T(8,128)(2,1)S(1)}, bf16[8,2048]{1,0:T(8,128)(2,1)S(1)}, u32[]{:S(2)}, u32[]{:S(2)}) collective-permute-start(bf16[8,2048]{1,0:T(8,128)(2,1)S(1)} %get-tuple-element.130), channel_id=1, source_target_pairs={{0,16},{16,32},{32,48},{48,64},{64,80},{80,96},{96,112},{112,128},... | collective-permute-start | bytes 98312 | tf_op jit(solution)/shard_map/ppermute | solution.py:232
  156.4 0.7 collective-permute-start.4
  180.3 0.7 collective-permute-start.5
  204.1 3.3 collective-permute-start.6
  231.2 11.9 %collective-permute-start.7 = (bf16[8,2048]{1,0:T(8,128)(2,1)S(1)}, bf16[8,2048]{1,0:T(8,128)(2,1)S(1)}, u32[]{:S(2)}, u32[]{:S(2)}) collective-permute-start(bf16[8,2048]{1,0:T(8,128)(2,1)S(1)} %get-tuple-element.154), channel_id=1, source_target_pairs={{0,16},{16,32},{32,48},{48,64},{64,80},{80,96},{96,112},{112,128},... | collective-permute-start | bytes 98312 | tf_op jit(solution)/shard_map/ppermute | solution.py:232
  267.5 0.7 collective-permute-start.8
  291.3 0.7 collective-permute-start.9
  315.2 3.3 collective-permute-start.10
  342.3 12.4 %collective-permute-start.11 = (bf16[8,2048]{1,0:T(8,128)(2,1)S(1)}, bf16[8,2048]{1,0:T(8,128)(2,1)S(1)}, u32[]{:S(2)}, u32[]{:S(2)}) collective-permute-start(bf16[8,2048]{1,0:T(8,128)(2,1)S(1)} %get-tuple-element.178), channel_id=1, source_target_pairs={{0,16},{16,32},{32,48},{48,64},{64,80},{80,96},{96,112},{112,128},... | collective-permute-start | bytes 98312 | tf_op jit(solution)/shard_map/ppermute | solution.py:232
  378.8 0.7 collective-permute-start.12
  402.7 0.7 collective-permute-start.13
  426.5 36.0 %collective-permute-start.14 = (bf16[8,2048]{1,0:T(8,128)(2,1)S(1)}, bf16[8,2048]{1,0:T(8,128)(2,1)S(1)}, u32[]{:S(2)}, u32[]{:S(2)}) collective-permute-start(bf16[8,2048]{1,0:T(8,128)(2,1)S(1)} %get-tuple-element.196), channel_id=1, source_target_pairs={{0,16},{16,32},{32,48},{48,0},{64,80},{80,96},{96,112},{112,64},{1... | collective-permute-start | bytes 98312 | tf_op jit(solution)/shard_map/ppermute | solution.py:232
  488.7 4.9 collective-permute-start.15
  508.6 11.9 %all-to-all-start.33 = ((bf16[16,32,128]{2,1,0:T(8,128)(2,1)}), bf16[16,32,128]{2,1,0:T(8,128)(2,1)S(1)}, u32[]{:S(2)}, u32[]{:S(2)}) async-start(bf16[16,32,128]{2,1,0:T(8,128)(2,1)} %get-tuple-element.206), calls=%async_computation.33 | async-start | bytes 262144 | tf_op jit(solution)/shard_map/all_to_all | solution.py:220
  (9 other events, 11.1 us)

commit v3 on v2

--- a/solution.py
+++ b/solution.py
@@ -145,13 +145,10 @@
 
 
 def onward(step, batches, sections):
-    row = 4 if sections % 4 == 0 else sections
     needed = [step - batch for batch in range(batches) if 0 <= step - batch < sections - 1]
-    if step % row < row - 2:
+    if step % 4 == 1:
         return [(place, place + 1) for place in needed]
-    if any((place + 1) % row == 0 for place in needed):
-        row = sections
-    return [(place, place - place % row + (place + 1) % row) for place in range(sections)]
+    return [(place, (place + 1) % sections) for place in range(sections)]
 
 
 def body(acts, norm_gain, gate_w, up_w, down_w, route_ids, route_probs):

time: 532 us -> 525 us (0.987)
  starting transfers between devices: 89.1 us -> 75.9 us
    ppermute x16, starting transfers between devices: 76.6 us -> 63.3 us  [body(): arrived = lax.ppermute(sent, 'section', onward(step, batches, sections))]
  transfers between devices with their start and end apart: 18 -> 18, of which waited for: 10 -> 14; matrix products, arithmetic and copies ran while one was open for 0% -> 0% of each run, Pallas kernels for 0% -> 0%
where the time goes in v3:
time: 525 us; the launch traced here: 515 us
  blocking collectives  383 us (73%)
  starting transfers between devices  75.9 us (14%)
  waiting for transfers between devices  32.8 us (6%)
  local copies, waits for them, and re-layouts  13 us (2%)
  Pallas kernels  7.35 us (1%)
    all_to_all x16, blocking collectives, body(): lax.all_to_all(outgoing, 'expert', split_axis=0, concat_axis=0, tiled=True)  194 us
    all_to_all x16, blocking collectives, body(): lax.all_to_all(output, 'expert', split_axis=0, concat_axis=0, tiled=True)  189 us
    ppermute x16, starting transfers between devices, body(): arrived = lax.ppermute(sent, 'section', onward(step, batches, sections))  63.3 us
    ppermute x16, waiting for transfers between devices, body(): arrived = lax.ppermute(sent, 'section', onward(step, batches, sections))  22.7 us
    unnamed x30, local copies, waits for them, and re-layouts  13 us
  transfers between devices with their start and end apart: 18, of which 14 were waited for; matrix products, arithmetic and copies ran while one was open for 0% of the time, Pallas kernels for 0%

profile of v3, /device:TPU:31, one launch (start us, length us, event | category | flops | bytes accessed | tf_op | source)
XLA Modules:
  0.0 514.9 jit_solution(179071989821097947)
XLA Ops:
  27.1 14.8 %all_to_all.170.back_ref = bf16[16,32,128]{2,1,0:T(8,128)(2,1)S(1)} all-to-all(bf16[16,32,128]{2,1,0:T(8,128)(2,1)S(1)} %get-tuple-element.109), channel_id=1, replica_groups=mesh['section'=16,'expert'=16] {'expert'}, dimensions={0} | all-to-all | bytes 262144 | tf_op jit(solution)/shard_map/all_to_all | solution.py:217
  45.3 12.3 %all_to_all.171.in_ref = bf16[16,32,128]{2,1,0:T(8,128)(2,1)S(1)} all-to-all(bf16[16,32,128]{2,1,0:T(8,128)(2,1)S(1)} %get-tuple-element.114), channel_id=1, replica_groups=mesh['section'=16,'expert'=16] {'expert'}, dimensions={0} | all-to-all | bytes 262144 | tf_op jit(solution)/shard_map/all_to_all | solution.py:206
  57.6 11.6 %all_to_all.172.back_ref = bf16[16,32,128]{2,1,0:T(8,128)(2,1)S(1)} all-to-all(bf16[16,32,128]{2,1,0:T(8,128)(2,1)S(1)} %get-tuple-element.116), channel_id=1, replica_groups=mesh['section'=16,'expert'=16] {'expert'}, dimensions={0} | all-to-all | bytes 262144 | tf_op jit(solution)/shard_map/all_to_all | solution.py:217
  69.8 11.6 %all_to_all.173.in_ref = bf16[16,32,128]{2,1,0:T(8,128)(2,1)S(1)} all-to-all(bf16[16,32,128]{2,1,0:T(8,128)(2,1)S(1)} %get-tuple-element.120), channel_id=1, replica_groups=mesh['section'=16,'expert'=16] {'expert'}, dimensions={0} | all-to-all | bytes 262144 | tf_op jit(solution)/shard_map/all_to_all | solution.py:206
  81.4 11.6 %all_to_all.174.back_ref = bf16[16,32,128]{2,1,0:T(8,128)(2,1)S(1)} all-to-all(bf16[16,32,128]{2,1,0:T(8,128)(2,1)S(1)} %get-tuple-element.122), channel_id=1, replica_groups=mesh['section'=16,'expert'=16] {'expert'}, dimensions={0} | all-to-all | bytes 262144 | tf_op jit(solution)/shard_map/all_to_all | solution.py:217
  104.1 12.4 %all_to_all.175.in_ref = bf16[16,32,128]{2,1,0:T(8,128)(2,1)S(1)} all-to-all(bf16[16,32,128]{2,1,0:T(8,128)(2,1)S(1)} %get-tuple-element.126), channel_id=1, replica_groups=mesh['section'=16,'expert'=16] {'expert'}, dimensions={0} | all-to-all | bytes 262144 | tf_op jit(solution)/shard_map/all_to_all | solution.py:206
  134.6 12.4 %all_to_all.177.in_ref = bf16[16,32,128]{2,1,0:T(8,128)(2,1)S(1)} all-to-all(bf16[16,32,128]{2,1,0:T(8,128)(2,1)S(1)} %get-tuple-element.132), channel_id=1, replica_groups=mesh['section'=16,'expert'=16] {'expert'}, dimensions={0} | all-to-all | bytes 262144 | tf_op jit(solution)/shard_map/all_to_all | solution.py:206
  165.0 12.4 %all_to_all.179.in_ref = bf16[16,32,128]{2,1,0:T(8,128)(2,1)S(1)} all-to-all(bf16[16,32,128]{2,1,0:T(8,128)(2,1)S(1)} %get-tuple-element.138), channel_id=1, replica_groups=mesh['section'=16,'expert'=16] {'expert'}, dimensions={0} | all-to-all | bytes 262144 | tf_op jit(solution)/shard_map/all_to_all | solution.py:206
  177.4 11.6 %all_to_all.180.back_ref = bf16[16,32,128]{2,1,0:T(8,128)(2,1)S(1)} all-to-all(bf16[16,32,128]{2,1,0:T(8,128)(2,1)S(1)} %get-tuple-element.140), channel_id=1, replica_groups=mesh['section'=16,'expert'=16] {'expert'}, dimensions={0} | all-to-all | bytes 262144 | tf_op jit(solution)/shard_map/all_to_all | solution.py:217
  189.7 11.6 %all_to_all.181.in_ref = bf16[16,32,128]{2,1,0:T(8,128)(2,1)S(1)} all-to-all(bf16[16,32,128]{2,1,0:T(8,128)(2,1)S(1)} %get-tuple-element.144), channel_id=1, replica_groups=mesh['section'=16,'expert'=16] {'expert'}, dimensions={0} | all-to-all | bytes 262144 | tf_op jit(solution)/shard_map/all_to_all | solution.py:206
  219.3 12.4 %all_to_all.183.in_ref = bf16[16,32,128]{2,1,0:T(8,128)(2,1)S(1)} all-to-all(bf16[16,32,128]{2,1,0:T(8,128)(2,1)S(1)} %get-tuple-element.150), channel_id=1, replica_groups=mesh['section'=16,'expert'=16] {'expert'}, dimensions={0} | all-to-all | bytes 262144 | tf_op jit(solution)/shard_map/all_to_all | solution.py:206
  231.7 11.6 %all_to_all.184.back_ref = bf16[16,32,128]{2,1,0:T(8,128)(2,1)S(1)} all-to-all(bf16[16,32,128]{2,1,0:T(8,128)(2,1)S(1)} %get-tuple-element.152), channel_id=1, replica_groups=mesh['section'=16,'expert'=16] {'expert'}, dimensions={0} | all-to-all | bytes 262144 | tf_op jit(solution)/shard_map/all_to_all | solution.py:217
  249.7 12.5 %all_to_all.185.in_ref = bf16[16,32,128]{2,1,0:T(8,128)(2,1)S(1)} all-to-all(bf16[16,32,128]{2,1,0:T(8,128)(2,1)S(1)} %get-tuple-element.156), channel_id=1, replica_groups=mesh['section'=16,'expert'=16] {'expert'}, dimensions={0} | all-to-all | bytes 262144 | tf_op jit(solution)/shard_map/all_to_all | solution.py:206
  262.2 11.6 %all_to_all.186.back_ref = bf16[16,32,128]{2,1,0:T(8,128)(2,1)S(1)} all-to-all(bf16[16,32,128]{2,1,0:T(8,128)(2,1)S(1)} %get-tuple-element.158), channel_id=1, replica_groups=mesh['section'=16,'expert'=16] {'expert'}, dimensions={0} | all-to-all | bytes 262144 | tf_op jit(solution)/shard_map/all_to_all | solution.py:217
  280.4 12.4 %all_to_all.187.in_ref = bf16[16,32,128]{2,1,0:T(8,128)(2,1)S(1)} all-to-all(bf16[16,32,128]{2,1,0:T(8,128)(2,1)S(1)} %get-tuple-element.162), channel_id=1, replica_groups=mesh['section'=16,'expert'=16] {'expert'}, dimensions={0} | all-to-all | bytes 262144 | tf_op jit(solution)/shard_map/all_to_all | solution.py:206
  305.1 11.6 %all_to_all.189.in_ref = bf16[16,32,128]{2,1,0:T(8,128)(2,1)S(1)} all-to-all(bf16[16,32,128]{2,1,0:T(8,128)(2,1)S(1)} %get-tuple-element.168), channel_id=1, replica_groups=mesh['section'=16,'expert'=16] {'expert'}, dimensions={0} | all-to-all | bytes 262144 | tf_op jit(solution)/shard_map/all_to_all | solution.py:206
  334.7 12.4 %all_to_all.191.in_ref = bf16[16,32,128]{2,1,0:T(8,128)(2,1)S(1)} all-to-all(bf16[16,32,128]{2,1,0:T(8,128)(2,1)S(1)} %get-tuple-element.174), channel_id=1, replica_groups=mesh['section'=16,'expert'=16] {'expert'}, dimensions={0} | all-to-all | bytes 262144 | tf_op jit(solution)/shard_map/all_to_all | solution.py:206
  365.1 12.4 %all_to_all.193.in_ref = bf16[16,32,128]{2,1,0:T(8,128)(2,1)S(1)} all-to-all(bf16[16,32,128]{2,1,0:T(8,128)(2,1)S(1)} %get-tuple-element.180), channel_id=1, replica_groups=mesh['section'=16,'expert'=16] {'expert'}, dimensions={0} | all-to-all | bytes 262144 | tf_op jit(solution)/shard_map/all_to_all | solution.py:206
  377.6 11.6 %all_to_all.194.back_ref = bf16[16,32,128]{2,1,0:T(8,128)(2,1)S(1)} all-to-all(bf16[16,32,128]{2,1,0:T(8,128)(2,1)S(1)} %get-tuple-element.182), channel_id=1, replica_groups=mesh['section'=16,'expert'=16] {'expert'}, dimensions={0} | all-to-all | bytes 262144 | tf_op jit(solution)/shard_map/all_to_all | solution.py:217
  395.6 12.4 %all_to_all.195.in_ref = bf16[16,32,128]{2,1,0:T(8,128)(2,1)S(1)} all-to-all(bf16[16,32,128]{2,1,0:T(8,128)(2,1)S(1)} %get-tuple-element.186), channel_id=1, replica_groups=mesh['section'=16,'expert'=16] {'expert'}, dimensions={0} | all-to-all | bytes 262144 | tf_op jit(solution)/shard_map/all_to_all | solution.py:206
  420.3 11.6 %all_to_all.197.in_ref = bf16[16,32,128]{2,1,0:T(8,128)(2,1)S(1)} all-to-all(bf16[16,32,128]{2,1,0:T(8,128)(2,1)S(1)} %get-tuple-element.192), channel_id=1, replica_groups=mesh['section'=16,'expert'=16] {'expert'}, dimensions={0} | all-to-all | bytes 262144 | tf_op jit(solution)/shard_map/all_to_all | solution.py:206
  456.2 12.1 %all_to_all.199.in_ref = bf16[16,32,128]{2,1,0:T(8,128)(2,1)S(1)} all-to-all(bf16[16,32,128]{2,1,0:T(8,128)(2,1)S(1)} %get-tuple-element.198), channel_id=1, replica_groups=mesh['section'=16,'expert'=16] {'expert'}, dimensions={0} | all-to-all | bytes 262144 | tf_op jit(solution)/shard_map/all_to_all | solution.py:206
  470.1 11.6 %all_to_all.200.back_ref = bf16[16,32,128]{2,1,0:T(8,128)(2,1)S(1)} all-to-all(bf16[16,32,128]{2,1,0:T(8,128)(2,1)S(1)} %get-tuple-element.200), channel_id=1, replica_groups=mesh['section'=16,'expert'=16] {'expert'}, dimensions={0} | all-to-all | bytes 262144 | tf_op jit(solution)/shard_map/all_to_all | solution.py:217
  487.3 12.1 %all_to_all.201.in_ref = bf16[16,32,128]{2,1,0:T(8,128)(2,1)S(1)} all-to-all(bf16[16,32,128]{2,1,0:T(8,128)(2,1)S(1)} %get-tuple-element.204), channel_id=1, replica_groups=mesh['section'=16,'expert'=16] {'expert'}, dimensions={0} | all-to-all | bytes 262144 | tf_op jit(solution)/shard_map/all_to_all | solution.py:206
  (128 shorter events, 223.5 us)
Async XLA Ops:
  5.0 18.3 %all-to-all-start = ((bf16[16,32,128]{2,1,0:T(8,128)(2,1)}), bf16[16,32,128]{2,1,0:T(8,128)(2,1)S(1)}, u32[]{:S(2)}, u32[]{:S(2)}) async-start(bf16[16,32,128]{2,1,0:T(8,128)(2,1)} %get-tuple-element.108), calls=%async_computation | async-start | bytes 262144 | tf_op jit(solution)/shard_map/all_to_all | solution.py:206
  19.8 3.5 copy-start.1
  23.3 1.9 copy-start.3
  27.1 14.9 %copy-start.12 = (bf16[8,2048]{1,0:T(8,128)(2,1)S(1)}, bf16[8,2048]{1,0:T(8,128)(2,1)}, u32[]{:S(2)}) copy-start(bf16[8,2048]{1,0:T(8,128)(2,1)} %copy-done.11) | copy-start | bytes 98308
  27.1 18.2 %copy-start.8 = (f32[1,2048]{1,0:T(1,128)S(1)}, f32[1,2048]{1,0:T(1,128)}, u32[]{:S(2)}) copy-start(f32[1,2048]{1,0:T(1,128)} %refs_1_.33) | copy-start | bytes 24580
  27.1 18.2 %copy-start.10 = (bf16[2,8,2048]{2,1,0:T(8,128)(2,1)S(1)}, bf16[2,8,2048]{2,1,0:T(8,128)(2,1)}, u32[]{:S(2)}) copy-start(bf16[2,8,2048]{2,1,0:T(8,128)(2,1)} %refs_1_.18) | copy-start | bytes 196612
  27.1 30.4 %copy-start.4 = (bf16[1,1,2048,768]{3,2,1,0:T(8,128)(2,1)S(1)}, bf16[1,1,2048,768]{3,2,1,0:T(8,128)(2,1)}, u32[]{:S(2)}) copy-start(bf16[1,1,2048,768]{3,2,1,0:T(8,128)(2,1)} %param.10) | copy-start | bytes 9437188
  42.0 3.3 collective-permute-start
  69.1 0.7 collective-permute-start.1
  93.0 11.1 %collective-permute-start.2 = (bf16[8,2048]{1,0:T(8,128)(2,1)S(1)}, bf16[8,2048]{1,0:T(8,128)(2,1)S(1)}, u32[]{:S(2)}, u32[]{:S(2)}) collective-permute-start(bf16[8,2048]{1,0:T(8,128)(2,1)S(1)} %get-tuple-element.124), channel_id=1, source_target_pairs={{0,16},{16,32},{32,48},{48,64},{64,80},{80,96},{96,112},{112,128},... | collective-permute-start | bytes 98312 | tf_op jit(solution)/shard_map/ppermute | solution.py:229
  128.1 6.6 %collective-permute-start.3 = (bf16[8,2048]{1,0:T(8,128)(2,1)S(1)}, bf16[8,2048]{1,0:T(8,128)(2,1)S(1)}, u32[]{:S(2)}, u32[]{:S(2)}) collective-permute-start(bf16[8,2048]{1,0:T(8,128)(2,1)S(1)} %get-tuple-element.130), channel_id=1, source_target_pairs={{0,16},{16,32},{32,48},{48,64},{64,80},{80,96},{96,112},{112,128},... | collective-permute-start | bytes 98312 | tf_op jit(solution)/shard_map/ppermute | solution.py:229
  158.6 6.4 %collective-permute-start.4 = (bf16[8,2048]{1,0:T(8,128)(2,1)S(1)}, bf16[8,2048]{1,0:T(8,128)(2,1)S(1)}, u32[]{:S(2)}, u32[]{:S(2)}) collective-permute-start(bf16[8,2048]{1,0:T(8,128)(2,1)S(1)} %get-tuple-element.136), channel_id=1, source_target_pairs={{0,16},{16,32},{32,48},{48,64},{64,80},{80,96},{96,112},{112,128},... | collective-permute-start | bytes 98312 | tf_op jit(solution)/shard_map/ppermute | solution.py:229
  189.0 0.7 collective-permute-start.5
  212.9 6.4 %collective-permute-start.6 = (bf16[8,2048]{1,0:T(8,128)(2,1)S(1)}, bf16[8,2048]{1,0:T(8,128)(2,1)S(1)}, u32[]{:S(2)}, u32[]{:S(2)}) collective-permute-start(bf16[8,2048]{1,0:T(8,128)(2,1)S(1)} %get-tuple-element.148), channel_id=1, source_target_pairs={{0,16},{16,32},{32,48},{48,64},{64,80},{80,96},{96,112},{112,128},... | collective-permute-start | bytes 98312 | tf_op jit(solution)/shard_map/ppermute | solution.py:229
  243.3 6.4 %collective-permute-start.7 = (bf16[8,2048]{1,0:T(8,128)(2,1)S(1)}, bf16[8,2048]{1,0:T(8,128)(2,1)S(1)}, u32[]{:S(2)}, u32[]{:S(2)}) collective-permute-start(bf16[8,2048]{1,0:T(8,128)(2,1)S(1)} %get-tuple-element.154), channel_id=1, source_target_pairs={{0,16},{16,32},{32,48},{48,64},{64,80},{80,96},{96,112},{112,128},... | collective-permute-start | bytes 98312 | tf_op jit(solution)/shard_map/ppermute | solution.py:229
  273.8 6.6 %collective-permute-start.8 = (bf16[8,2048]{1,0:T(8,128)(2,1)S(1)}, bf16[8,2048]{1,0:T(8,128)(2,1)S(1)}, u32[]{:S(2)}, u32[]{:S(2)}) collective-permute-start(bf16[8,2048]{1,0:T(8,128)(2,1)S(1)} %get-tuple-element.160), channel_id=1, source_target_pairs={{0,16},{16,32},{32,48},{48,64},{64,80},{80,96},{96,112},{112,128},... | collective-permute-start | bytes 98312 | tf_op jit(solution)/shard_map/ppermute | solution.py:229
  304.4 0.7 collective-permute-start.9
  328.2 6.4 %collective-permute-start.10 = (bf16[8,2048]{1,0:T(8,128)(2,1)S(1)}, bf16[8,2048]{1,0:T(8,128)(2,1)S(1)}, u32[]{:S(2)}, u32[]{:S(2)}) collective-permute-start(bf16[8,2048]{1,0:T(8,128)(2,1)S(1)} %get-tuple-element.172), channel_id=1, source_target_pairs={{0,16},{16,32},{32,48},{48,64},{64,80},{80,96},{96,112},{112,128},... | collective-permute-start | bytes 98312 | tf_op jit(solution)/shard_map/ppermute | solution.py:229
  358.6 6.4 %collective-permute-start.11 = (bf16[8,2048]{1,0:T(8,128)(2,1)S(1)}, bf16[8,2048]{1,0:T(8,128)(2,1)S(1)}, u32[]{:S(2)}, u32[]{:S(2)}) collective-permute-start(bf16[8,2048]{1,0:T(8,128)(2,1)S(1)} %get-tuple-element.178), channel_id=1, source_target_pairs={{0,16},{16,32},{32,48},{48,64},{64,80},{80,96},{96,112},{112,128},... | collective-permute-start | bytes 98312 | tf_op jit(solution)/shard_map/ppermute | solution.py:229
  389.2 6.4 %collective-permute-start.12 = (bf16[8,2048]{1,0:T(8,128)(2,1)S(1)}, bf16[8,2048]{1,0:T(8,128)(2,1)S(1)}, u32[]{:S(2)}, u32[]{:S(2)}) collective-permute-start(bf16[8,2048]{1,0:T(8,128)(2,1)S(1)} %get-tuple-element.184), channel_id=1, source_target_pairs={{0,16},{16,32},{32,48},{48,64},{64,80},{80,96},{96,112},{112,128},... | collective-permute-start | bytes 98312 | tf_op jit(solution)/shard_map/ppermute | solution.py:229
  419.6 0.7 collective-permute-start.13
  443.5 12.3 %collective-permute-start.14 = (bf16[8,2048]{1,0:T(8,128)(2,1)S(1)}, bf16[8,2048]{1,0:T(8,128)(2,1)S(1)}, u32[]{:S(2)}, u32[]{:S(2)}) collective-permute-start(bf16[8,2048]{1,0:T(8,128)(2,1)S(1)} %get-tuple-element.196), channel_id=1, source_target_pairs={{0,16},{16,32},{32,48},{48,64},{64,80},{80,96},{96,112},{112,128},... | collective-permute-start | bytes 98312 | tf_op jit(solution)/shard_map/ppermute | solution.py:229
  481.9 5.0 collective-permute-start.15
  501.9 11.9 %all-to-all-start.33 = ((bf16[16,32,128]{2,1,0:T(8,128)(2,1)}), bf16[16,32,128]{2,1,0:T(8,128)(2,1)S(1)}, u32[]{:S(2)}, u32[]{:S(2)}) async-start(bf16[16,32,128]{2,1,0:T(8,128)(2,1)} %get-tuple-element.206), calls=%async_computation.33 | async-start | bytes 262144 | tf_op jit(solution)/shard_map/all_to_all | solution.py:217
  (9 other events, 11.1 us)

commit v4 on v3

--- a/solution.py
+++ b/solution.py
@@ -48,35 +48,81 @@
     return jnp.concatenate(parts, axis=0)
 
 
-def weights_kernel(*refs):
-    hidden_ref = refs[-1]
-    hidden_ref[...] = jnp.zeros_like(hidden_ref)
-
-
-def tables_kernel(owners, ids_ref, probs_ref, send_ref, take_ref, layer_ref):
-    layer_ref[...] = jnp.zeros_like(layer_ref)
-    batches, picks, tokens = ids_ref.shape
+def stay(value):
+    return pltpu.with_memory_space_constraint(value, pltpu.HBM)
+
+
+def copies(sources, targets, sems):
+    return [
+        pltpu.make_async_copy(source, target, sems.at[place])
+        for place, (source, target) in enumerate(zip(sources, targets))
+    ]
+
+
+def slot_tables(owners, ids, probs):
+    picks, tokens = ids.shape
     experts = lax.broadcasted_iota(jnp.int32, (owners, tokens), 0)
     earlier = (
         lax.broadcasted_iota(jnp.int32, (tokens, tokens), 0)
         < lax.broadcasted_iota(jnp.int32, (tokens, tokens), 1)
     ).astype(BF16)
-    for batch in range(batches):
-        ids = ids_ref[batch]
-        probs = probs_ref[batch]
-        named = jnp.zeros((owners, tokens), F32)
-        weight = jnp.zeros((owners, tokens), F32)
-        for pick in range(picks):
-            hit = ids[pick : pick + 1, :] == experts
-            named = named + jnp.where(hit, 1.0, 0.0)
-            weight = weight + jnp.where(hit, probs[pick : pick + 1, :], 0.0)
-        slot = jnp.dot(named.astype(BF16), earlier, preferred_element_type=F32)
-        split = [jnp.abs(slot - number) < 0.5 for number in range(SLOTS)]
-        send = jnp.concatenate([jnp.where(own, named, 0.0) for own in split], axis=0)
-        take = jnp.concatenate([jnp.where(own, weight, 0.0) for own in split], axis=0)
-        send_ref[batch] = send.astype(BF16)
-        high = take.astype(BF16).astype(F32)
-        take_ref[batch] = jnp.concatenate([high, take - high], axis=1).astype(BF16)
+    named = jnp.zeros((owners, tokens), F32)
+    weight = jnp.zeros((owners, tokens), F32)
+    for pick in range(picks):
+        hit = ids[pick : pick + 1, :] == experts
+        named = named + jnp.where(hit, 1.0, 0.0)
+        weight = weight + jnp.where(hit, probs[pick : pick + 1, :], 0.0)
+    slot = jnp.dot(named.astype(BF16), earlier, preferred_element_type=F32)
+    split = [jnp.abs(slot - number) < 0.5 for number in range(SLOTS)]
+    send = jnp.concatenate([jnp.where(own, named, 0.0) for own in split], axis=0)
+    take = jnp.concatenate([jnp.where(own, weight, 0.0) for own in split], axis=0)
+    high = take.astype(BF16).astype(F32)
+    return send.astype(BF16), jnp.concatenate([high, take - high], axis=1).astype(BF16)
+
+
+def dispatch_rows(x, gain, send, out_ref, spare):
+    wide = x.astype(F32)
+    mean = jnp.mean(wide * wide, axis=-1, keepdims=True)
+    normed = (wide * lax.rsqrt(mean + 1e-06) * gain).astype(BF16)
+    rows = jnp.dot(send, normed, preferred_element_type=F32)
+    spread_rows(rows, spare, out_ref.shape[0])
+    out_ref[...] = spare[...].astype(BF16).reshape(out_ref.shape)
+
+
+def first_kernel(
+    ids_hbm,
+    probs_hbm,
+    acts_hbm,
+    gain_hbm,
+    _gate,
+    _up,
+    _down,
+    out_ref,
+    acts_ref,
+    gain_ref,
+    send_ref,
+    take_ref,
+    hidden_ref,
+    layer_ref,
+    ids_ref,
+    probs_ref,
+    spare,
+    sems,
+):
+    moves = copies(
+        (ids_hbm, probs_hbm, acts_hbm, gain_hbm), (ids_ref, probs_ref, acts_ref, gain_ref), sems
+    )
+    for move in moves:
+        move.start()
+    for ref in (hidden_ref, layer_ref):
+        ref[...] = jnp.zeros_like(ref)
+    for move in moves:
+        move.wait()
+    for batch in range(ids_ref.shape[0]):
+        send_ref[batch], take_ref[batch] = slot_tables(
+            out_ref.shape[0], ids_ref[batch], probs_ref[batch]
+        )
+    dispatch_rows(acts_ref[0], gain_ref[...], send_ref[0], out_ref, spare)
 
 
 def when_active(step, batches):
@@ -88,24 +134,16 @@
     return call
 
 
-def dispatch_kernel(step, owners, batches, *refs):
-    *sources, gain_ref, send_ref, out_ref, x_ref, spare = refs
+def dispatch_kernel(step, batches, *refs):
+    arrived_ref, *acts, gain_ref, send_ref, out_ref, x_ref, spare = refs
 
     @when_active(step, batches)
     def _(held):
-        if step == 0:
-            x = sources[0][0]
-        elif step < batches:
-            x = jnp.where(held == step, sources[1][step], sources[0][...])
-        else:
-            x = sources[0][...]
+        x = arrived_ref[...]
+        if acts:
+            x = jnp.where(held == step, acts[0][step], x)
         x_ref[...] = x
-        wide = x.astype(F32)
-        mean = jnp.mean(wide * wide, axis=-1, keepdims=True)
-        normed = (wide * lax.rsqrt(mean + 1e-06) * gain_ref[...]).astype(BF16)
-        rows = jnp.dot(send_ref[held], normed, preferred_element_type=F32)
-        spread_rows(rows, spare, owners)
-        out_ref[...] = spare[...].astype(BF16).reshape(out_ref.shape)
+        dispatch_rows(x, gain_ref[...], send_ref[held], out_ref, spare)
 
 
 def expert_kernel(step, batches, in_ref, gate_ref, up_ref, down_ref, _, out_ref, hidden_ref, spare):
@@ -128,7 +166,7 @@
     step, batches, last, x_ref, back_ref, take_ref, before_ref, sent_ref, out_ref, spare
 ):
     owners, height, lanes = back_ref.shape
-    tokens = x_ref.shape[0]
+    tokens = x_ref.shape[-2]
     if last:
         out_ref[...] = before_ref[...]
 
@@ -139,7 +177,8 @@
         mixed = lax.dot_general(
             take_ref[held], rows, (((0,), (0,)), ((), ())), preferred_element_type=F32
         )
-        result = x_ref[...].astype(F32) + (mixed[:tokens] + mixed[tokens:])
+        x = x_ref[...] if step > 0 else x_ref[0]
+        result = x.astype(F32) + (mixed[:tokens] + mixed[tokens:])
         sent_ref[...] = result.astype(BF16)
         out_ref[held] = result
 
@@ -160,49 +199,53 @@
     steps = batches + sections - 1
     height = SLOTS * feature // LANES
     scale = 2.0 / (batches * tokens * picks)
-    w_gate, w_up, w_down = gate_w[0, 0], up_w[0, 0], down_w[0, 0]
+    weights = (gate_w[0, 0], up_w[0, 0], down_w[0, 0])
     packed = jax.ShapeDtypeStruct((owners, height, LANES), BF16)
     held_x = jax.ShapeDtypeStruct((tokens, feature), BF16)
     hidden_shape = jax.ShapeDtypeStruct((batches, SLOTS * owners, hidden_width), BF16)
     layer_shape = jax.ShapeDtypeStruct((batches, tokens, feature), F32)
     spare = [pltpu.VMEM((owners * height, LANES), F32)]
 
-    hiddens = pl.pallas_call(
-        weights_kernel,
-        out_shape=hidden_shape,
-        in_specs=[vmem()] * 3,
-        out_specs=vmem(),
-        compiler_params=params(2),
-        cost_estimate=pl.CostEstimate(
-            flops=0, bytes_accessed=4 * 3 * w_gate.size, transcendentals=0
-        ),
-        name="weights",
-    )(w_gate, w_up, w_down)
-    send, take, layer_out = pl.pallas_call(
-        functools.partial(tables_kernel, owners),
+    hbm = pl.BlockSpec(memory_space=pltpu.HBM)
+    ids = jnp.swapaxes(route_ids[0], 1, 2)
+    probs = jnp.swapaxes(route_probs[0], 1, 2)
+    outgoing, local_acts, gain, send, take, hiddens, layer_out = pl.pallas_call(
+        first_kernel,
         out_shape=(
+            packed,
+            jax.ShapeDtypeStruct(acts.shape, acts.dtype),
+            jax.ShapeDtypeStruct(norm_gain.shape, norm_gain.dtype),
             jax.ShapeDtypeStruct((batches, SLOTS * owners, tokens), BF16),
             jax.ShapeDtypeStruct((batches, SLOTS * owners, 2 * tokens), BF16),
+            hidden_shape,
             layer_shape,
         ),
-        in_specs=[vmem()] * 2,
-        out_specs=(vmem(),) * 3,
+        in_specs=[hbm] * 7,
+        out_specs=(vmem(),) * 7,
+        scratch_shapes=[
+            pltpu.VMEM(ids.shape, ids.dtype),
+            pltpu.VMEM(probs.shape, probs.dtype),
+            *spare,
+            pltpu.SemaphoreType.DMA((4,)),
+        ],
         compiler_params=params(2),
-        name="tables",
-    )(jnp.swapaxes(route_ids[0], 1, 2), jnp.swapaxes(route_probs[0], 1, 2))
-
-    sources = [acts]
+        name="first",
+    )(*map(stay, (ids, probs, acts, norm_gain, *weights)))
+    wide = local_acts
+
     for step in range(steps):
         last = step == steps - 1
-        outgoing, wide = pl.pallas_call(
-            functools.partial(dispatch_kernel, step, owners, batches),
-            out_shape=(packed, held_x),
-            in_specs=[vmem()] * (len(sources) + 2),
-            out_specs=(vmem(), vmem()),
-            scratch_shapes=spare,
-            compiler_params=params(2),
-            name="dispatch",
-        )(*sources, norm_gain, send)
+        if step > 0:
+            sources = [arrived, local_acts] if step < batches else [arrived]
+            outgoing, wide = pl.pallas_call(
+                functools.partial(dispatch_kernel, step, batches),
+                out_shape=(packed, held_x),
+                in_specs=[vmem()] * (len(sources) + 2),
+                out_specs=(vmem(), vmem()),
+                scratch_shapes=spare,
+                compiler_params=params(2),
+                name="dispatch",
+            )(*sources, gain, send)
         incoming = lax.all_to_all(outgoing, "expert", split_axis=0, concat_axis=0, tiled=True)
         output, hiddens = pl.pallas_call(
             functools.partial(expert_kernel, step, batches),
@@ -213,7 +256,7 @@
             input_output_aliases={4: 1},
             compiler_params=params(2),
             name="expert",
-        )(incoming, w_gate, w_up, w_down, hiddens)
+        )(incoming, *weights, hiddens)
         back = lax.all_to_all(output, "expert", split_axis=0, concat_axis=0, tiled=True)
         sent, layer_out = pl.pallas_call(
             functools.partial(combine_kernel, step, batches, last),
@@ -227,7 +270,6 @@
         )(wide, back, take, layer_out)
         if not last:
             arrived = lax.ppermute(sent, "section", onward(step, batches, sections))
-            sources = [arrived, acts] if step + 1 < batches else [arrived]
     rows = hiddens.reshape(batches * SLOTS * owners, hidden_width)
     square = lax.dot_general(rows, rows, (((0,), (0,)), ((), ())), preferred_element_type=F32)
     return (layer_out[None], (scale * square)[None, None])

time: 525 us -> 515 us (0.981)
  blocking collectives: 383 us -> 398 us
  local copies, waits for them, and re-layouts: 13 us -> 0.01 us
  starting transfers between devices: 75.9 us -> 66.4 us
    all_to_all x16 -> x17, blocking collectives: 194 us -> 213 us  [body(): lax.all_to_all(outgoing, 'expert', split_axis=0, concat_axis=0, tiled=True)]
    unnamed x30 -> x6, local copies, waits for them, and re-layouts: 13 us -> 0.01 us
    all_to_all x1 -> x0, starting transfers between devices: 9.15 us -> none  [body(): lax.all_to_all(outgoing, 'expert', split_axis=0, concat_axis=0, tiled=True)]
  transfers between devices with their start and end apart: 18 -> 17, of which waited for: 14 -> 13; matrix products, arithmetic and copies ran while one was open for 0% -> 0% of each run, Pallas kernels for 0% -> 0%
where the time goes in v4:
time: 515 us; the launch traced here: 505 us
  blocking collectives  398 us (77%)
  starting transfers between devices  66.4 us (13%)
  waiting for transfers between devices  29.3 us (6%)
  Pallas kernels  8.12 us (2%)
    all_to_all x17, blocking collectives, body(): lax.all_to_all(outgoing, 'expert', split_axis=0, concat_axis=0, tiled=True)  213 us
    all_to_all x16, blocking collectives, body(): lax.all_to_all(output, 'expert', split_axis=0, concat_axis=0, tiled=True)  185 us
    ppermute x16, starting transfers between devices, body(): arrived = lax.ppermute(sent, 'section', onward(step, batches, sections))  63 us
    ppermute x16, waiting for transfers between devices, body(): arrived = lax.ppermute(sent, 'section', onward(step, batches, sections))  22.8 us
  transfers between devices with their start and end apart: 17, of which 13 were waited for; matrix products, arithmetic and copies ran while one was open for 0% of the time, Pallas kernels for 0%

profile of v4, /device:TPU:31, one launch (start us, length us, event | category | flops | bytes accessed | tf_op | source)
XLA Modules:
  0.0 504.9 jit_solution(3944818195223519412)
XLA Ops:
  2.1 18.4 %all_to_all.170.in_ref = bf16[16,32,128]{2,1,0:T(8,128)(2,1)S(1)} all-to-all(bf16[16,32,128]{2,1,0:T(8,128)(2,1)S(1)} %get-tuple-element.109), channel_id=1, replica_groups=mesh['section'=16,'expert'=16] {'expert'}, dimensions={0} | all-to-all | bytes 262144 | tf_op jit(solution)/shard_map/all_to_all | solution.py:249
  20.6 11.6 %all_to_all.171.back_ref = bf16[16,32,128]{2,1,0:T(8,128)(2,1)S(1)} all-to-all(bf16[16,32,128]{2,1,0:T(8,128)(2,1)S(1)} %get-tuple-element.111), channel_id=1, replica_groups=mesh['section'=16,'expert'=16] {'expert'}, dimensions={0} | all-to-all | bytes 262144 | tf_op jit(solution)/shard_map/all_to_all | solution.py:260
  35.4 12.2 %all_to_all.172.in_ref = bf16[16,32,128]{2,1,0:T(8,128)(2,1)S(1)} all-to-all(bf16[16,32,128]{2,1,0:T(8,128)(2,1)S(1)} %get-tuple-element.118), channel_id=1, replica_groups=mesh['section'=16,'expert'=16] {'expert'}, dimensions={0} | all-to-all | bytes 262144 | tf_op jit(solution)/shard_map/all_to_all | solution.py:249
  59.9 11.6 %all_to_all.174.in_ref = bf16[16,32,128]{2,1,0:T(8,128)(2,1)S(1)} all-to-all(bf16[16,32,128]{2,1,0:T(8,128)(2,1)S(1)} %get-tuple-element.124), channel_id=1, replica_groups=mesh['section'=16,'expert'=16] {'expert'}, dimensions={0} | all-to-all | bytes 262144 | tf_op jit(solution)/shard_map/all_to_all | solution.py:249
  94.1 12.4 %all_to_all.176.in_ref = bf16[16,32,128]{2,1,0:T(8,128)(2,1)S(1)} all-to-all(bf16[16,32,128]{2,1,0:T(8,128)(2,1)S(1)} %get-tuple-element.130), channel_id=1, replica_groups=mesh['section'=16,'expert'=16] {'expert'}, dimensions={0} | all-to-all | bytes 262144 | tf_op jit(solution)/shard_map/all_to_all | solution.py:249
  106.5 11.6 %all_to_all.177.back_ref = bf16[16,32,128]{2,1,0:T(8,128)(2,1)S(1)} all-to-all(bf16[16,32,128]{2,1,0:T(8,128)(2,1)S(1)} %get-tuple-element.132), channel_id=1, replica_groups=mesh['section'=16,'expert'=16] {'expert'}, dimensions={0} | all-to-all | bytes 262144 | tf_op jit(solution)/shard_map/all_to_all | solution.py:260
  124.7 12.4 %all_to_all.178.in_ref = bf16[16,32,128]{2,1,0:T(8,128)(2,1)S(1)} all-to-all(bf16[16,32,128]{2,1,0:T(8,128)(2,1)S(1)} %get-tuple-element.136), channel_id=1, replica_groups=mesh['section'=16,'expert'=16] {'expert'}, dimensions={0} | all-to-all | bytes 262144 | tf_op jit(solution)/shard_map/all_to_all | solution.py:249
  155.1 12.4 %all_to_all.180.in_ref = bf16[16,32,128]{2,1,0:T(8,128)(2,1)S(1)} all-to-all(bf16[16,32,128]{2,1,0:T(8,128)(2,1)S(1)} %get-tuple-element.142), channel_id=1, replica_groups=mesh['section'=16,'expert'=16] {'expert'}, dimensions={0} | all-to-all | bytes 262144 | tf_op jit(solution)/shard_map/all_to_all | solution.py:249
  167.5 11.6 %all_to_all.181.back_ref = bf16[16,32,128]{2,1,0:T(8,128)(2,1)S(1)} all-to-all(bf16[16,32,128]{2,1,0:T(8,128)(2,1)S(1)} %get-tuple-element.144), channel_id=1, replica_groups=mesh['section'=16,'expert'=16] {'expert'}, dimensions={0} | all-to-all | bytes 262144 | tf_op jit(solution)/shard_map/all_to_all | solution.py:260
  179.7 11.6 %all_to_all.182.in_ref = bf16[16,32,128]{2,1,0:T(8,128)(2,1)S(1)} all-to-all(bf16[16,32,128]{2,1,0:T(8,128)(2,1)S(1)} %get-tuple-element.148), channel_id=1, replica_groups=mesh['section'=16,'expert'=16] {'expert'}, dimensions={0} | all-to-all | bytes 262144 | tf_op jit(solution)/shard_map/all_to_all | solution.py:249
  209.4 12.4 %all_to_all.184.in_ref = bf16[16,32,128]{2,1,0:T(8,128)(2,1)S(1)} all-to-all(bf16[16,32,128]{2,1,0:T(8,128)(2,1)S(1)} %get-tuple-element.154), channel_id=1, replica_groups=mesh['section'=16,'expert'=16] {'expert'}, dimensions={0} | all-to-all | bytes 262144 | tf_op jit(solution)/shard_map/all_to_all | solution.py:249
  221.7 11.6 %all_to_all.185.back_ref = bf16[16,32,128]{2,1,0:T(8,128)(2,1)S(1)} all-to-all(bf16[16,32,128]{2,1,0:T(8,128)(2,1)S(1)} %get-tuple-element.156), channel_id=1, replica_groups=mesh['section'=16,'expert'=16] {'expert'}, dimensions={0} | all-to-all | bytes 262144 | tf_op jit(solution)/shard_map/all_to_all | solution.py:260
  239.7 12.5 %all_to_all.186.in_ref = bf16[16,32,128]{2,1,0:T(8,128)(2,1)S(1)} all-to-all(bf16[16,32,128]{2,1,0:T(8,128)(2,1)S(1)} %get-tuple-element.160), channel_id=1, replica_groups=mesh['section'=16,'expert'=16] {'expert'}, dimensions={0} | all-to-all | bytes 262144 | tf_op jit(solution)/shard_map/all_to_all | solution.py:249
  252.3 11.6 %all_to_all.187.back_ref = bf16[16,32,128]{2,1,0:T(8,128)(2,1)S(1)} all-to-all(bf16[16,32,128]{2,1,0:T(8,128)(2,1)S(1)} %get-tuple-element.162), channel_id=1, replica_groups=mesh['section'=16,'expert'=16] {'expert'}, dimensions={0} | all-to-all | bytes 262144 | tf_op jit(solution)/shard_map/all_to_all | solution.py:260
  270.5 12.4 %all_to_all.188.in_ref = bf16[16,32,128]{2,1,0:T(8,128)(2,1)S(1)} all-to-all(bf16[16,32,128]{2,1,0:T(8,128)(2,1)S(1)} %get-tuple-element.166), channel_id=1, replica_groups=mesh['section'=16,'expert'=16] {'expert'}, dimensions={0} | all-to-all | bytes 262144 | tf_op jit(solution)/shard_map/all_to_all | solution.py:249
  295.1 11.6 %all_to_all.190.in_ref = bf16[16,32,128]{2,1,0:T(8,128)(2,1)S(1)} all-to-all(bf16[16,32,128]{2,1,0:T(8,128)(2,1)S(1)} %get-tuple-element.172), channel_id=1, replica_groups=mesh['section'=16,'expert'=16] {'expert'}, dimensions={0} | all-to-all | bytes 262144 | tf_op jit(solution)/shard_map/all_to_all | solution.py:249
  324.7 12.4 %all_to_all.192.in_ref = bf16[16,32,128]{2,1,0:T(8,128)(2,1)S(1)} all-to-all(bf16[16,32,128]{2,1,0:T(8,128)(2,1)S(1)} %get-tuple-element.178), channel_id=1, replica_groups=mesh['section'=16,'expert'=16] {'expert'}, dimensions={0} | all-to-all | bytes 262144 | tf_op jit(solution)/shard_map/all_to_all | solution.py:249
  355.1 12.4 %all_to_all.194.in_ref = bf16[16,32,128]{2,1,0:T(8,128)(2,1)S(1)} all-to-all(bf16[16,32,128]{2,1,0:T(8,128)(2,1)S(1)} %get-tuple-element.184), channel_id=1, replica_groups=mesh['section'=16,'expert'=16] {'expert'}, dimensions={0} | all-to-all | bytes 262144 | tf_op jit(solution)/shard_map/all_to_all | solution.py:249
  367.7 11.6 %all_to_all.195.back_ref = bf16[16,32,128]{2,1,0:T(8,128)(2,1)S(1)} all-to-all(bf16[16,32,128]{2,1,0:T(8,128)(2,1)S(1)} %get-tuple-element.186), channel_id=1, replica_groups=mesh['section'=16,'expert'=16] {'expert'}, dimensions={0} | all-to-all | bytes 262144 | tf_op jit(solution)/shard_map/all_to_all | solution.py:260
  385.7 12.4 %all_to_all.196.in_ref = bf16[16,32,128]{2,1,0:T(8,128)(2,1)S(1)} all-to-all(bf16[16,32,128]{2,1,0:T(8,128)(2,1)S(1)} %get-tuple-element.190), channel_id=1, replica_groups=mesh['section'=16,'expert'=16] {'expert'}, dimensions={0} | all-to-all | bytes 262144 | tf_op jit(solution)/shard_map/all_to_all | solution.py:249
  410.3 11.6 %all_to_all.198.in_ref = bf16[16,32,128]{2,1,0:T(8,128)(2,1)S(1)} all-to-all(bf16[16,32,128]{2,1,0:T(8,128)(2,1)S(1)} %get-tuple-element.196), channel_id=1, replica_groups=mesh['section'=16,'expert'=16] {'expert'}, dimensions={0} | all-to-all | bytes 262144 | tf_op jit(solution)/shard_map/all_to_all | solution.py:249
  446.2 12.1 %all_to_all.200.in_ref = bf16[16,32,128]{2,1,0:T(8,128)(2,1)S(1)} all-to-all(bf16[16,32,128]{2,1,0:T(8,128)(2,1)S(1)} %get-tuple-element.202), channel_id=1, replica_groups=mesh['section'=16,'expert'=16] {'expert'}, dimensions={0} | all-to-all | bytes 262144 | tf_op jit(solution)/shard_map/all_to_all | solution.py:249
  460.1 11.6 %all_to_all.201.back_ref = bf16[16,32,128]{2,1,0:T(8,128)(2,1)S(1)} all-to-all(bf16[16,32,128]{2,1,0:T(8,128)(2,1)S(1)} %get-tuple-element.204), channel_id=1, replica_groups=mesh['section'=16,'expert'=16] {'expert'}, dimensions={0} | all-to-all | bytes 262144 | tf_op jit(solution)/shard_map/all_to_all | solution.py:260
  477.3 12.1 %all_to_all.202.in_ref = bf16[16,32,128]{2,1,0:T(8,128)(2,1)S(1)} all-to-all(bf16[16,32,128]{2,1,0:T(8,128)(2,1)S(1)} %get-tuple-element.208), channel_id=1, replica_groups=mesh['section'=16,'expert'=16] {'expert'}, dimensions={0} | all-to-all | bytes 262144 | tf_op jit(solution)/shard_map/all_to_all | solution.py:249
  (101 shorter events, 210.0 us)
Async XLA Ops:
  0.6 19.9 %copy-start = (bf16[1,1,2048,768]{3,2,1,0:T(8,128)(2,1)S(1)}, bf16[1,1,2048,768]{3,2,1,0:T(8,128)(2,1)}, u32[]{:S(2)}) copy-start(bf16[1,1,2048,768]{3,2,1,0:T(8,128)(2,1)} %param.9) | copy-start | bytes 9437188
  0.6 19.9 %copy-start.1 = (bf16[1,1,2048,768]{3,2,1,0:T(8,128)(2,1)S(1)}, bf16[1,1,2048,768]{3,2,1,0:T(8,128)(2,1)}, u32[]{:S(2)}) copy-start(bf16[1,1,2048,768]{3,2,1,0:T(8,128)(2,1)} %param.10) | copy-start | bytes 9437188
  0.7 19.9 %copy-start.2 = (bf16[1,1,768,2048]{3,2,1,0:T(8,128)(2,1)S(1)}, bf16[1,1,768,2048]{3,2,1,0:T(8,128)(2,1)}, u32[]{:S(2)}) copy-start(bf16[1,1,768,2048]{3,2,1,0:T(8,128)(2,1)} %param.11) | copy-start | bytes 9437188
  32.2 3.3 collective-permute-start
  59.2 0.7 collective-permute-start.1
  83.1 11.0 %collective-permute-start.2 = (bf16[8,2048]{1,0:T(8,128)(2,1)S(1)}, bf16[8,2048]{1,0:T(8,128)(2,1)S(1)}, u32[]{:S(2)}, u32[]{:S(2)}) collective-permute-start(bf16[8,2048]{1,0:T(8,128)(2,1)S(1)} %get-tuple-element.128), channel_id=1, source_target_pairs={{0,16},{16,32},{32,48},{48,64},{64,80},{80,96},{96,112},{112,128},... | collective-permute-start | bytes 98312 | tf_op jit(solution)/shard_map/ppermute | solution.py:272
  118.1 6.4 %collective-permute-start.3 = (bf16[8,2048]{1,0:T(8,128)(2,1)S(1)}, bf16[8,2048]{1,0:T(8,128)(2,1)S(1)}, u32[]{:S(2)}, u32[]{:S(2)}) collective-permute-start(bf16[8,2048]{1,0:T(8,128)(2,1)S(1)} %get-tuple-element.134), channel_id=1, source_target_pairs={{0,16},{16,32},{32,48},{48,64},{64,80},{80,96},{96,112},{112,128},... | collective-permute-start | bytes 98312 | tf_op jit(solution)/shard_map/ppermute | solution.py:272
  148.7 6.4 %collective-permute-start.4 = (bf16[8,2048]{1,0:T(8,128)(2,1)S(1)}, bf16[8,2048]{1,0:T(8,128)(2,1)S(1)}, u32[]{:S(2)}, u32[]{:S(2)}) collective-permute-start(bf16[8,2048]{1,0:T(8,128)(2,1)S(1)} %get-tuple-element.140), channel_id=1, source_target_pairs={{0,16},{16,32},{32,48},{48,64},{64,80},{80,96},{96,112},{112,128},... | collective-permute-start | bytes 98312 | tf_op jit(solution)/shard_map/ppermute | solution.py:272
  179.1 0.7 collective-permute-start.5
  202.9 6.4 %collective-permute-start.6 = (bf16[8,2048]{1,0:T(8,128)(2,1)S(1)}, bf16[8,2048]{1,0:T(8,128)(2,1)S(1)}, u32[]{:S(2)}, u32[]{:S(2)}) collective-permute-start(bf16[8,2048]{1,0:T(8,128)(2,1)S(1)} %get-tuple-element.152), channel_id=1, source_target_pairs={{0,16},{16,32},{32,48},{48,64},{64,80},{80,96},{96,112},{112,128},... | collective-permute-start | bytes 98312 | tf_op jit(solution)/shard_map/ppermute | solution.py:272
  233.3 6.4 %collective-permute-start.7 = (bf16[8,2048]{1,0:T(8,128)(2,1)S(1)}, bf16[8,2048]{1,0:T(8,128)(2,1)S(1)}, u32[]{:S(2)}, u32[]{:S(2)}) collective-permute-start(bf16[8,2048]{1,0:T(8,128)(2,1)S(1)} %get-tuple-element.158), channel_id=1, source_target_pairs={{0,16},{16,32},{32,48},{48,64},{64,80},{80,96},{96,112},{112,128},... | collective-permute-start | bytes 98312 | tf_op jit(solution)/shard_map/ppermute | solution.py:272
  263.9 6.6 %collective-permute-start.8 = (bf16[8,2048]{1,0:T(8,128)(2,1)S(1)}, bf16[8,2048]{1,0:T(8,128)(2,1)S(1)}, u32[]{:S(2)}, u32[]{:S(2)}) collective-permute-start(bf16[8,2048]{1,0:T(8,128)(2,1)S(1)} %get-tuple-element.164), channel_id=1, source_target_pairs={{0,16},{16,32},{32,48},{48,64},{64,80},{80,96},{96,112},{112,128},... | collective-permute-start | bytes 98312 | tf_op jit(solution)/shard_map/ppermute | solution.py:272
  294.4 0.7 collective-permute-start.9
  318.3 6.4 %collective-permute-start.10 = (bf16[8,2048]{1,0:T(8,128)(2,1)S(1)}, bf16[8,2048]{1,0:T(8,128)(2,1)S(1)}, u32[]{:S(2)}, u32[]{:S(2)}) collective-permute-start(bf16[8,2048]{1,0:T(8,128)(2,1)S(1)} %get-tuple-element.176), channel_id=1, source_target_pairs={{0,16},{16,32},{32,48},{48,64},{64,80},{80,96},{96,112},{112,128},... | collective-permute-start | bytes 98312 | tf_op jit(solution)/shard_map/ppermute | solution.py:272
  348.7 6.4 %collective-permute-start.11 = (bf16[8,2048]{1,0:T(8,128)(2,1)S(1)}, bf16[8,2048]{1,0:T(8,128)(2,1)S(1)}, u32[]{:S(2)}, u32[]{:S(2)}) collective-permute-start(bf16[8,2048]{1,0:T(8,128)(2,1)S(1)} %get-tuple-element.182), channel_id=1, source_target_pairs={{0,16},{16,32},{32,48},{48,64},{64,80},{80,96},{96,112},{112,128},... | collective-permute-start | bytes 98312 | tf_op jit(solution)/shard_map/ppermute | solution.py:272
  379.3 6.4 %collective-permute-start.12 = (bf16[8,2048]{1,0:T(8,128)(2,1)S(1)}, bf16[8,2048]{1,0:T(8,128)(2,1)S(1)}, u32[]{:S(2)}, u32[]{:S(2)}) collective-permute-start(bf16[8,2048]{1,0:T(8,128)(2,1)S(1)} %get-tuple-element.188), channel_id=1, source_target_pairs={{0,16},{16,32},{32,48},{48,64},{64,80},{80,96},{96,112},{112,128},... | collective-permute-start | bytes 98312 | tf_op jit(solution)/shard_map/ppermute | solution.py:272
  409.6 0.7 collective-permute-start.13
  433.5 12.3 %collective-permute-start.14 = (bf16[8,2048]{1,0:T(8,128)(2,1)S(1)}, bf16[8,2048]{1,0:T(8,128)(2,1)S(1)}, u32[]{:S(2)}, u32[]{:S(2)}) collective-permute-start(bf16[8,2048]{1,0:T(8,128)(2,1)S(1)} %get-tuple-element.200), channel_id=1, source_target_pairs={{0,16},{16,32},{32,48},{48,64},{64,80},{80,96},{96,112},{112,128},... | collective-permute-start | bytes 98312 | tf_op jit(solution)/shard_map/ppermute | solution.py:272
  472.0 5.0 collective-permute-start.15
  491.9 11.9 %all-to-all-start.33 = ((bf16[16,32,128]{2,1,0:T(8,128)(2,1)}), bf16[16,32,128]{2,1,0:T(8,128)(2,1)S(1)}, u32[]{:S(2)}, u32[]{:S(2)}) async-start(bf16[16,32,128]{2,1,0:T(8,128)(2,1)} %get-tuple-element.210), calls=%async_computation.33 | async-start | bytes 262144 | tf_op jit(solution)/shard_map/all_to_all | solution.py:260

commit v5 on v4

--- a/solution.py
+++ b/solution.py
@@ -185,9 +185,26 @@
 
 def onward(step, batches, sections):
     needed = [step - batch for batch in range(batches) if 0 <= step - batch < sections - 1]
-    if step % 4 == 1:
+    if step in (1, 5):
         return [(place, place + 1) for place in needed]
     return [(place, (place + 1) % sections) for place in range(sections)]
+
+
+def groups_of(step, batches, sections, owners):
+    row = 4 if sections % 4 == 0 and owners % 4 == 0 else 1
+    lots = owners // row
+    working = {(step - batch) // row for batch in range(batches)}
+    groups = []
+    for first in range(0, sections, row):
+        places = range(first, first + row)
+        if first // row in working:
+            groups += [[place * owners + own for own in range(owners)] for place in places]
+        else:
+            groups += [
+                [place * owners + lot * lots + own for place in places for own in range(lots)]
+                for lot in range(row)
+            ]
+    return groups
 
 
 def body(acts, norm_gain, gate_w, up_w, down_w, route_ids, route_probs):
@@ -246,7 +263,10 @@
                 compiler_params=params(2),
                 name="dispatch",
             )(*sources, gain, send)
-        incoming = lax.all_to_all(outgoing, "expert", split_axis=0, concat_axis=0, tiled=True)
+        incoming = lax.all_to_all(
+            outgoing, ("section", "expert"), split_axis=0, concat_axis=0, tiled=True,
+            axis_index_groups=groups_of(step, batches, sections, owners),
+        )
         output, hiddens = pl.pallas_call(
             functools.partial(expert_kernel, step, batches),
             out_shape=(packed, hidden_shape),
@@ -257,7 +277,10 @@
             compiler_params=params(2),
             name="expert",
         )(incoming, *weights, hiddens)
-        back = lax.all_to_all(output, "expert", split_axis=0, concat_axis=0, tiled=True)
+        back = lax.all_to_all(
+            output, ("section", "expert"), split_axis=0, concat_axis=0, tiled=True,
+            axis_index_groups=groups_of(step, batches, sections, owners),
+        )
         sent, layer_out = pl.pallas_call(
             functools.partial(combine_kernel, step, batches, last),
             out_shape=(held_x, layer_shape),

time: 515 us -> 515 us (level)
  the two profiles are of different devices: /device:TPU:31 before, /device:TPU:25 now
where the time goes in v5:
time: 515 us; the launch traced here: 505 us
  blocking collectives  398 us (77%)
  waiting for transfers between devices  88.7 us (17%)
  Pallas kernels  7.92 us (2%)
  starting transfers between devices  7.65 us (1%)
    all_to_all x17, blocking collectives, body(): lax.all_to_all(outgoing, ('section', 'expert'), split_axis=0, concat_axis...  240 us
    all_to_all x16, blocking collectives, body(): lax.all_to_all(output, ('section', 'expert'), split_axis=0, concat_axis=0...  158 us
    ppermute x16, waiting for transfers between devices, body(): arrived = lax.ppermute(sent, 'section', onward(step, batches, sections))  82.2 us
  transfers between devices with their start and end apart: 17, of which 15 were waited for; matrix products, arithmetic and copies ran while one was open for 0% of the time, Pallas kernels for 0%

profile of v5, /device:TPU:25, one launch (start us, length us, event | category | flops | bytes accessed | tf_op | source)
XLA Modules:
  0.0 505.1 jit_solution(2155102383488230529)
XLA Ops:
  2.1 12.5 %all_to_all.170.in_ref = bf16[16,32,128]{2,1,0:T(8,128)(2,1)S(1)} all-to-all(bf16[16,32,128]{2,1,0:T(8,128)(2,1)S(1)} %get-tuple-element.109), channel_id=1, replica_groups={{0,1,2,3,4,5,6,7,8,9,10,11,12,13,14,15},{16,17,18,19,20,21,22,23,24,25,..., dimensions={0} | all-to-all | bytes 262144 | tf_op jit(solution)/shard_map/all_to_all | solution.py:266
  28.9 16.8 %all_to_all.172.in_ref = bf16[16,32,128]{2,1,0:T(8,128)(2,1)S(1)} all-to-all(bf16[16,32,128]{2,1,0:T(8,128)(2,1)S(1)} %get-tuple-element.118), channel_id=1, replica_groups={{0,1,2,3,4,5,6,7,8,9,10,11,12,13,14,15},{16,17,18,19,20,21,22,23,24,25,..., dimensions={0} | all-to-all | bytes 262144 | tf_op jit(solution)/shard_map/all_to_all | solution.py:266
  55.7 9.3 %all_to_all.174.in_ref = bf16[16,32,128]{2,1,0:T(8,128)(2,1)S(1)} all-to-all(bf16[16,32,128]{2,1,0:T(8,128)(2,1)S(1)} %get-tuple-element.124), channel_id=1, replica_groups={{0,1,2,3,4,5,6,7,8,9,10,11,12,13,14,15},{16,17,18,19,20,21,22,23,24,25,..., dimensions={0} | all-to-all | bytes 262144 | tf_op jit(solution)/shard_map/all_to_all | solution.py:266
  65.0 9.3 %all_to_all.175.back_ref = bf16[16,32,128]{2,1,0:T(8,128)(2,1)S(1)} all-to-all(bf16[16,32,128]{2,1,0:T(8,128)(2,1)S(1)} %get-tuple-element.126), channel_id=1, replica_groups={{0,1,2,3,4,5,6,7,8,9,10,11,12,13,14,15},{16,17,18,19,20,21,22,23,24,25,..., dimensions={0} | all-to-all | bytes 262144 | tf_op jit(solution)/shard_map/all_to_all | solution.py:280
  79.2 25.4 %all_to_all.176.in_ref = bf16[16,32,128]{2,1,0:T(8,128)(2,1)S(1)} all-to-all(bf16[16,32,128]{2,1,0:T(8,128)(2,1)S(1)} %get-tuple-element.130), channel_id=1, replica_groups={{0,1,2,3,4,5,6,7,8,9,10,11,12,13,14,15},{16,17,18,19,20,21,22,23,24,25,..., dimensions={0} | all-to-all | bytes 262144 | tf_op jit(solution)/shard_map/all_to_all | solution.py:266
  118.9 16.3 %all_to_all.178.in_ref = bf16[16,32,128]{2,1,0:T(8,128)(2,1)S(1)} all-to-all(bf16[16,32,128]{2,1,0:T(8,128)(2,1)S(1)} %get-tuple-element.136), channel_id=1, replica_groups={{0,1,2,3,4,5,6,7,8,9,10,11,12,13,14,15},{16,17,18,19,20,21,22,23,24,25,..., dimensions={0} | all-to-all | bytes 262144 | tf_op jit(solution)/shard_map/all_to_all | solution.py:266
  149.4 16.2 %all_to_all.180.in_ref = bf16[16,32,128]{2,1,0:T(8,128)(2,1)S(1)} all-to-all(bf16[16,32,128]{2,1,0:T(8,128)(2,1)S(1)} %get-tuple-element.142), channel_id=1, replica_groups={{0,1,2,3,16,17,18,19,32,33,34,35,48,49,50,51},{4,5,6,7,20,21,22,23,36,3..., dimensions={0} | all-to-all | bytes 262144 | tf_op jit(solution)/shard_map/all_to_all | solution.py:266
  175.6 9.3 %all_to_all.182.in_ref = bf16[16,32,128]{2,1,0:T(8,128)(2,1)S(1)} all-to-all(bf16[16,32,128]{2,1,0:T(8,128)(2,1)S(1)} %get-tuple-element.148), channel_id=1, replica_groups={{0,1,2,3,16,17,18,19,32,33,34,35,48,49,50,51},{4,5,6,7,20,21,22,23,36,3..., dimensions={0} | all-to-all | bytes 262144 | tf_op jit(solution)/shard_map/all_to_all | solution.py:266
  184.9 9.3 %all_to_all.183.back_ref = bf16[16,32,128]{2,1,0:T(8,128)(2,1)S(1)} all-to-all(bf16[16,32,128]{2,1,0:T(8,128)(2,1)S(1)} %get-tuple-element.150), channel_id=1, replica_groups={{0,1,2,3,16,17,18,19,32,33,34,35,48,49,50,51},{4,5,6,7,20,21,22,23,36,3..., dimensions={0} | all-to-all | bytes 262144 | tf_op jit(solution)/shard_map/all_to_all | solution.py:280
  199.1 11.9 %all_to_all.184.in_ref = bf16[16,32,128]{2,1,0:T(8,128)(2,1)S(1)} all-to-all(bf16[16,32,128]{2,1,0:T(8,128)(2,1)S(1)} %get-tuple-element.154), channel_id=1, replica_groups={{0,1,2,3,16,17,18,19,32,33,34,35,48,49,50,51},{4,5,6,7,20,21,22,23,36,3..., dimensions={0} | all-to-all | bytes 262144 | tf_op jit(solution)/shard_map/all_to_all | solution.py:266
  225.1 18.9 %all_to_all.186.in_ref = bf16[16,32,128]{2,1,0:T(8,128)(2,1)S(1)} all-to-all(bf16[16,32,128]{2,1,0:T(8,128)(2,1)S(1)} %get-tuple-element.160), channel_id=1, replica_groups={{0,1,2,3,16,17,18,19,32,33,34,35,48,49,50,51},{4,5,6,7,20,21,22,23,36,3..., dimensions={0} | all-to-all | bytes 262144 | tf_op jit(solution)/shard_map/all_to_all | solution.py:266
  258.1 15.5 %all_to_all.188.in_ref = bf16[16,32,128]{2,1,0:T(8,128)(2,1)S(1)} all-to-all(bf16[16,32,128]{2,1,0:T(8,128)(2,1)S(1)} %get-tuple-element.166), channel_id=1, replica_groups={{0,1,2,3,16,17,18,19,32,33,34,35,48,49,50,51},{4,5,6,7,20,21,22,23,36,3..., dimensions={0} | all-to-all | bytes 262144 | tf_op jit(solution)/shard_map/all_to_all | solution.py:266
  287.7 15.4 %all_to_all.190.in_ref = bf16[16,32,128]{2,1,0:T(8,128)(2,1)S(1)} all-to-all(bf16[16,32,128]{2,1,0:T(8,128)(2,1)S(1)} %get-tuple-element.172), channel_id=1, replica_groups={{0,1,2,3,16,17,18,19,32,33,34,35,48,49,50,51},{4,5,6,7,20,21,22,23,36,3..., dimensions={0} | all-to-all | bytes 262144 | tf_op jit(solution)/shard_map/all_to_all | solution.py:266
  317.2 11.7 %all_to_all.192.in_ref = bf16[16,32,128]{2,1,0:T(8,128)(2,1)S(1)} all-to-all(bf16[16,32,128]{2,1,0:T(8,128)(2,1)S(1)} %get-tuple-element.178), channel_id=1, replica_groups={{0,1,2,3,16,17,18,19,32,33,34,35,48,49,50,51},{4,5,6,7,20,21,22,23,36,3..., dimensions={0} | all-to-all | bytes 262144 | tf_op jit(solution)/shard_map/all_to_all | solution.py:266
  338.6 18.9 %collective-permute-done.11.refs_0_ = bf16[8,2048]{1,0:T(8,128)(2,1)S(1)} collective-permute-done((bf16[8,2048]{1,0:T(8,128)(2,1)S(1)}, bf16[8,2048]{1,0:T(8,128)(2,1)S(1)}, u32[]{:S(2)}, u32[]{:S(2)}) %collective-permute-start.11) | collective-permute-done | bytes 32800 | tf_op jit(solution)/shard_map/ppermute | solution.py:295
  357.9 12.1 %all_to_all.194.in_ref = bf16[16,32,128]{2,1,0:T(8,128)(2,1)S(1)} all-to-all(bf16[16,32,128]{2,1,0:T(8,128)(2,1)S(1)} %get-tuple-element.184), channel_id=1, replica_groups={{0,1,2,3,16,17,18,19,32,33,34,35,48,49,50,51},{4,5,6,7,20,21,22,23,36,3..., dimensions={0} | all-to-all | bytes 262144 | tf_op jit(solution)/shard_map/all_to_all | solution.py:266
  371.8 11.6 %all_to_all.195.back_ref = bf16[16,32,128]{2,1,0:T(8,128)(2,1)S(1)} all-to-all(bf16[16,32,128]{2,1,0:T(8,128)(2,1)S(1)} %get-tuple-element.186), channel_id=1, replica_groups={{0,1,2,3,16,17,18,19,32,33,34,35,48,49,50,51},{4,5,6,7,20,21,22,23,36,3..., dimensions={0} | all-to-all | bytes 262144 | tf_op jit(solution)/shard_map/all_to_all | solution.py:280
  389.6 12.1 %all_to_all.196.in_ref = bf16[16,32,128]{2,1,0:T(8,128)(2,1)S(1)} all-to-all(bf16[16,32,128]{2,1,0:T(8,128)(2,1)S(1)} %get-tuple-element.190), channel_id=1, replica_groups={{0,1,2,3,16,17,18,19,32,33,34,35,48,49,50,51},{4,5,6,7,20,21,22,23,36,3..., dimensions={0} | all-to-all | bytes 262144 | tf_op jit(solution)/shard_map/all_to_all | solution.py:266
  403.5 11.6 %all_to_all.197.back_ref = bf16[16,32,128]{2,1,0:T(8,128)(2,1)S(1)} all-to-all(bf16[16,32,128]{2,1,0:T(8,128)(2,1)S(1)} %get-tuple-element.192), channel_id=1, replica_groups={{0,1,2,3,16,17,18,19,32,33,34,35,48,49,50,51},{4,5,6,7,20,21,22,23,36,3..., dimensions={0} | all-to-all | bytes 262144 | tf_op jit(solution)/shard_map/all_to_all | solution.py:280
  420.8 12.2 %all_to_all.198.in_ref = bf16[16,32,128]{2,1,0:T(8,128)(2,1)S(1)} all-to-all(bf16[16,32,128]{2,1,0:T(8,128)(2,1)S(1)} %get-tuple-element.196), channel_id=1, replica_groups={{0,1,2,3,16,17,18,19,32,33,34,35,48,49,50,51},{4,5,6,7,20,21,22,23,36,3..., dimensions={0} | all-to-all | bytes 262144 | tf_op jit(solution)/shard_map/all_to_all | solution.py:266
  433.1 11.6 %all_to_all.199.back_ref = bf16[16,32,128]{2,1,0:T(8,128)(2,1)S(1)} all-to-all(bf16[16,32,128]{2,1,0:T(8,128)(2,1)S(1)} %get-tuple-element.198), channel_id=1, replica_groups={{0,1,2,3,16,17,18,19,32,33,34,35,48,49,50,51},{4,5,6,7,20,21,22,23,36,3..., dimensions={0} | all-to-all | bytes 262144 | tf_op jit(solution)/shard_map/all_to_all | solution.py:280
  450.0 12.2 %all_to_all.200.in_ref = bf16[16,32,128]{2,1,0:T(8,128)(2,1)S(1)} all-to-all(bf16[16,32,128]{2,1,0:T(8,128)(2,1)S(1)} %get-tuple-element.202), channel_id=1, replica_groups={{0,1,2,3,16,17,18,19,32,33,34,35,48,49,50,51},{4,5,6,7,20,21,22,23,36,3..., dimensions={0} | all-to-all | bytes 262144 | tf_op jit(solution)/shard_map/all_to_all | solution.py:266
  462.2 11.6 %all_to_all.201.back_ref = bf16[16,32,128]{2,1,0:T(8,128)(2,1)S(1)} all-to-all(bf16[16,32,128]{2,1,0:T(8,128)(2,1)S(1)} %get-tuple-element.204), channel_id=1, replica_groups={{0,1,2,3,16,17,18,19,32,33,34,35,48,49,50,51},{4,5,6,7,20,21,22,23,36,3..., dimensions={0} | all-to-all | bytes 262144 | tf_op jit(solution)/shard_map/all_to_all | solution.py:280
  479.4 12.2 %all_to_all.202.in_ref = bf16[16,32,128]{2,1,0:T(8,128)(2,1)S(1)} all-to-all(bf16[16,32,128]{2,1,0:T(8,128)(2,1)S(1)} %get-tuple-element.208), channel_id=1, replica_groups={{0,1,2,3,16,17,18,19,32,33,34,35,48,49,50,51},{4,5,6,7,20,21,22,23,36,3..., dimensions={0} | all-to-all | bytes 262144 | tf_op jit(solution)/shard_map/all_to_all | solution.py:266
  (101 shorter events, 180.1 us)
Async XLA Ops:
  0.6 14.1 %copy-start = (bf16[1,1,2048,768]{3,2,1,0:T(8,128)(2,1)S(1)}, bf16[1,1,2048,768]{3,2,1,0:T(8,128)(2,1)}, u32[]{:S(2)}) copy-start(bf16[1,1,2048,768]{3,2,1,0:T(8,128)(2,1)} %param.9) | copy-start | bytes 9437188
  0.6 14.1 %copy-start.1 = (bf16[1,1,2048,768]{3,2,1,0:T(8,128)(2,1)S(1)}, bf16[1,1,2048,768]{3,2,1,0:T(8,128)(2,1)}, u32[]{:S(2)}) copy-start(bf16[1,1,2048,768]{3,2,1,0:T(8,128)(2,1)} %param.10) | copy-start | bytes 9437188
  0.7 14.0 %copy-start.2 = (bf16[1,1,768,2048]{3,2,1,0:T(8,128)(2,1)S(1)}, bf16[1,1,768,2048]{3,2,1,0:T(8,128)(2,1)}, u32[]{:S(2)}) copy-start(bf16[1,1,768,2048]{3,2,1,0:T(8,128)(2,1)} %param.11) | copy-start | bytes 9437188
  24.0 4.9 collective-permute-start
  55.0 0.7 collective-permute-start.1
  74.3 4.9 collective-permute-start.2
  113.9 4.9 collective-permute-start.3
  144.5 4.9 collective-permute-start.4
  174.9 0.7 collective-permute-start.5
  194.2 4.9 collective-permute-start.6
  220.2 4.9 collective-permute-start.7
  253.2 4.9 collective-permute-start.8
  282.9 4.9 collective-permute-start.9
  312.4 4.9 collective-permute-start.10
  338.2 19.3 %collective-permute-start.11 = (bf16[8,2048]{1,0:T(8,128)(2,1)S(1)}, bf16[8,2048]{1,0:T(8,128)(2,1)S(1)}, u32[]{:S(2)}, u32[]{:S(2)}) collective-permute-start(bf16[8,2048]{1,0:T(8,128)(2,1)S(1)} %get-tuple-element.182), channel_id=1, source_target_pairs={{0,16},{16,32},{32,48},{48,64},{64,80},{80,96},{96,112},{112,128},... | collective-permute-start | bytes 98312 | tf_op jit(solution)/shard_map/ppermute | solution.py:295
  383.6 5.6 %collective-permute-start.12 = (bf16[8,2048]{1,0:T(8,128)(2,1)S(1)}, bf16[8,2048]{1,0:T(8,128)(2,1)S(1)}, u32[]{:S(2)}, u32[]{:S(2)}) collective-permute-start(bf16[8,2048]{1,0:T(8,128)(2,1)S(1)} %get-tuple-element.188), channel_id=1, source_target_pairs={{0,16},{16,32},{32,48},{48,64},{64,80},{80,96},{96,112},{112,128},... | collective-permute-start | bytes 98312 | tf_op jit(solution)/shard_map/ppermute | solution.py:295
  415.4 5.5 %collective-permute-start.13 = (bf16[8,2048]{1,0:T(8,128)(2,1)S(1)}, bf16[8,2048]{1,0:T(8,128)(2,1)S(1)}, u32[]{:S(2)}, u32[]{:S(2)}) collective-permute-start(bf16[8,2048]{1,0:T(8,128)(2,1)S(1)} %get-tuple-element.194), channel_id=1, source_target_pairs={{0,16},{16,32},{32,48},{48,64},{64,80},{80,96},{96,112},{112,128},... | collective-permute-start | bytes 98312 | tf_op jit(solution)/shard_map/ppermute | solution.py:295
  444.6 5.4 %collective-permute-start.14 = (bf16[8,2048]{1,0:T(8,128)(2,1)S(1)}, bf16[8,2048]{1,0:T(8,128)(2,1)S(1)}, u32[]{:S(2)}, u32[]{:S(2)}) collective-permute-start(bf16[8,2048]{1,0:T(8,128)(2,1)S(1)} %get-tuple-element.200), channel_id=1, source_target_pairs={{0,16},{16,32},{32,48},{48,64},{64,80},{80,96},{96,112},{112,128},... | collective-permute-start | bytes 98312 | tf_op jit(solution)/shard_map/ppermute | solution.py:295
  473.8 5.6 %collective-permute-start.15 = (bf16[8,2048]{1,0:T(8,128)(2,1)S(1)}, bf16[8,2048]{1,0:T(8,128)(2,1)S(1)}, u32[]{:S(2)}, u32[]{:S(2)}) collective-permute-start(bf16[8,2048]{1,0:T(8,128)(2,1)S(1)} %get-tuple-element.206), channel_id=1, source_target_pairs={{0,16},{16,32},{32,48},{48,64},{64,80},{80,96},{96,112},{112,128},... | collective-permute-start | bytes 98312 | tf_op jit(solution)/shard_map/ppermute | solution.py:295
  492.3 11.9 %all-to-all-start.33 = ((bf16[16,32,128]{2,1,0:T(8,128)(2,1)}), bf16[16,32,128]{2,1,0:T(8,128)(2,1)S(1)}, u32[]{:S(2)}, u32[]{:S(2)}) async-start(bf16[16,32,128]{2,1,0:T(8,128)(2,1)} %get-tuple-element.210), calls=%async_computation.33 | async-start | bytes 262144 | tf_op jit(solution)/shard_map/all_to_all | solution.py:280
